TPU v7x, 32 devices: a whole 2x2x4 slice. The times are simulated.
32 devices in a mesh: dp: 8 (over y, x, core), tensor: 4 (over z).
Axes of the slice: x: 2, y: 2, z: 4, core: 2. Of those that a mesh axis runs over, the one named last changes fastest.
Arguments:
- residual_in: bfloat16 [1024, 7168], P('dp', 'tensor'), may hold values from -6 to 6
- queries: bfloat16 [1024, 64, 192], P('dp', 'tensor'), may hold values from -41 to 41
- latent: bfloat16 [1024, 576], P('dp'), may hold values from -6 to 6
- latent_up: bfloat16 [64, 512, 256], P('tensor'), may hold values from -0.25 to 0.25
- out_proj: bfloat16 [8192, 7168], P('tensor', 'dp'), may hold values from -0.0625 to 0.0625
- norm_gain: bfloat16 [7168], P('tensor'), may hold values from 0.099609375 to 1.8984375
- expert_ids: int32 [1024, 8], P('dp'), may hold values from 0 to 255, all different within a row; in each aligned block of 128 rows (0 to 127, 128 to 255, ...) at most 8 rows name the same one
- gate_num: int32 [1024, 8], P('dp'), may hold values from 16 to 256
- slot_table: int32 [256], replicated, may hold values from 0 to 255, each once
- gate_proj: bfloat16 [8, 7168, 1024], P('dp', 'tensor'), may hold values from -0.0625 to 0.0625
- up_proj: bfloat16 [8, 7168, 1024], P('dp', 'tensor'), may hold values from -0.0625 to 0.0625
- down_proj: bfloat16 [8, 1024, 7168], P('dp', 'tensor'), may hold values from -0.1875 to 0.1875
- inv_chol: float32 [8, 1024, 128], P('dp', 'tensor'), as said below
Outputs:
- residual_out: bfloat16 [1024, 7168], P('dp', 'tensor')
- moe_out: bfloat16 [1024, 7168], P('dp', 'tensor')
- down_quant: bfloat16 [8, 1024, 7168], P('dp', 'tensor')
- panel_gram: float32 [8, 1024, 128], P('dp', 'tensor')
Inputs may be any that keep to these rules, and one draw needn't show every extreme that they name: `expert_ids`: in the rows of one sequence of 128 tokens no expert is named by more than 8 rows; a row names 8 different experts. `slot_table`: each number of 0 to 255 appears once. `inv_chol`: each 128 x 128 block along the second dimension is upper triangular with a positive diagonal of at least one half.
All inputs are finite; a program needn't handle non-finite values.
Results may differ from a plain program's by a relative error of at most 0.039.
Values may be sent and summed in bfloat16 or wider, within the bound.
No kernel may reach another device: no remote copies, remote signals or barrier semaphores. Data moves between devices by JAX's collectives and lax.ppermute only.
A program may use at most 256 MiB of HBM per device.

v0:
```python
import math

import jax
import jax.numpy as jnp
from jax import lax
from jax.sharding import PartitionSpec as P

D = 7168
NOPE = 128
ROPE = 64
VHEAD = 128
LATENT = 512
PANEL = 128
BLK = 16
CAP = 8


def soft_levels(values, low, step):
    scaled = jnp.clip((values - low) / step, 0.0, 15.0)
    return low + step * (scaled - jnp.sin(2.0 * math.pi * scaled) / (2.0 * math.pi))


def quantize_panel(weight, upper):
    low = jnp.min(weight, axis=0)
    high = jnp.max(weight, axis=0)
    step = (high - low) / 15.0 + 1e-05
    strict = jnp.triu(upper, 1)
    diagonal = jnp.diagonal(upper)
    remaining = weight
    finished = []
    for begin in range(0, weight.shape[0], BLK):
        current = [remaining[offset] for offset in range(BLK)]
        remaining = remaining[BLK:]
        errors = []
        for offset in range(BLK):
            column = begin + offset
            levels = soft_levels(current[offset], low, step)
            finished.append(levels)
            error = (current[offset] - levels) / diagonal[column]
            errors.append(error)
            for later in range(offset + 1, BLK):
                current[later] = current[later] - strict[column, begin + later] * error
        if remaining.shape[0] > 0:
            coupling = strict[begin : begin + BLK, begin + BLK :]
            remaining = remaining - jnp.dot(
                coupling.T, jnp.stack(errors), precision=lax.Precision.HIGHEST
            )
    return jnp.stack(finished)


def shards(
    residual_in,
    queries,
    latent,
    latent_up,
    out_proj,
    norm_gain,
    expert_ids,
    gate_num,
    slot_table,
    gate_proj,
    up_proj,
    down_proj,
    inv_chol,
):
    seq_len = queries.shape[0]
    head_count = queries.shape[1]
    scale = 1.0 / math.sqrt(NOPE + ROPE)
    key_value = jnp.einsum(
        "tc,hcd->thd", latent[:, :LATENT], latent_up, preferred_element_type=jnp.float32
    ).astype(jnp.bfloat16)
    rotary = jnp.broadcast_to(latent[:, None, LATENT:], (seq_len, head_count, ROPE))
    keys = jnp.concatenate([key_value[:, :, :NOPE], rotary], axis=2)
    scores = jnp.einsum("thd,shd->hts", queries, keys, preferred_element_type=jnp.float32) * scale
    causal = jnp.arange(seq_len)[None, :] <= jnp.arange(seq_len)[:, None]
    scores = jnp.where(causal[None], scores, -1e30)
    top = jnp.max(scores, axis=2, keepdims=True)
    expo = jnp.exp(scores - top)
    probs = (expo / jnp.sum(expo, axis=2, keepdims=True)).astype(jnp.bfloat16)
    result = jnp.einsum(
        "hts,shd->thd", probs, key_value[:, :, NOPE:], preferred_element_type=jnp.float32
    )
    attended = result.astype(jnp.bfloat16).reshape(seq_len, head_count * VHEAD)
    partial_out = jnp.dot(
        attended,
        lax.all_gather(out_proj, "dp", axis=1, tiled=True),
        preferred_element_type=jnp.float32,
    )
    attn = lax.psum_scatter(
        partial_out.astype(jnp.bfloat16), "tensor", scatter_dimension=1, tiled=True
    ).astype(jnp.float32)
    residual_out = (residual_in.astype(jnp.float32) + attn).astype(jnp.bfloat16)
    wide = residual_out.astype(jnp.float32)
    square_tot = lax.psum(jnp.sum(wide * wide, axis=1), "tensor")
    normed = (
        wide * lax.rsqrt(square_tot / D + 1e-06)[:, None] * norm_gain.astype(jnp.float32)
    ).astype(jnp.bfloat16)
    owners = lax.axis_size("dp")
    capacity = CAP
    experts_all = slot_table.shape[0]
    flat_ids = expert_ids.reshape(-1)
    table_hit = flat_ids[:, None] == jnp.arange(experts_all, dtype=jnp.int32)[None, :]
    slots = jnp.sum(jnp.where(table_hit, slot_table[None, :], 0), axis=1)
    onehot = (slots[:, None] == jnp.arange(owners, dtype=jnp.int32)[None, :]).astype(jnp.int32)
    before = jnp.cumsum(onehot, axis=0) - onehot
    position = jnp.sum(before * onehot, axis=1)
    target = jnp.where(slots < owners, slots * capacity + position, -1)
    select = jnp.arange(owners * capacity, dtype=jnp.int32)[:, None] == target[None, :]
    pick_any = jnp.sum(
        select.astype(jnp.float32).reshape(owners * capacity, seq_len, -1), axis=2
    ).astype(jnp.bfloat16)
    gate_frac = gate_num.reshape(-1).astype(jnp.float32) / 256.0
    combine = jnp.sum(
        jnp.where(select, gate_frac[None, :], 0.0).reshape(owners * capacity, seq_len, -1), axis=2
    ).astype(jnp.bfloat16)
    outgoing = (
        jnp.dot(pick_any, normed, preferred_element_type=jnp.float32)
        .astype(jnp.bfloat16)
        .reshape(owners, capacity, -1)
    )
    incoming = lax.all_to_all(outgoing, "dp", split_axis=0, concat_axis=0, tiled=True)
    routed = incoming.reshape(owners * capacity, -1)
    gate_part = jnp.dot(routed, gate_proj[0], preferred_element_type=jnp.float32)
    up_part = jnp.dot(routed, up_proj[0], preferred_element_type=jnp.float32)
    gate_val, up_val = (
        lax.psum_scatter(
            gate_part.astype(jnp.bfloat16), "tensor", scatter_dimension=1, tiled=True
        ).astype(jnp.float32),
        lax.psum_scatter(
            up_part.astype(jnp.bfloat16), "tensor", scatter_dimension=1, tiled=True
        ).astype(jnp.float32),
    )
    hidden = (jax.nn.silu(gate_val) * up_val).astype(jnp.bfloat16)
    unit_count = hidden.shape[1]
    panel_count = unit_count // PANEL
    split = hidden.reshape(-1, panel_count, PANEL)
    gram = (
        jnp.einsum("rpi,rpj->pij", split, split, preferred_element_type=jnp.float32)
        / routed.shape[0]
    )
    panels = down_proj[0].astype(jnp.float32).reshape(panel_count, PANEL, -1)
    uppers = inv_chol[0].reshape(panel_count, PANEL, PANEL)
    quantized = (
        jax.vmap(quantize_panel)(panels, uppers).reshape(unit_count, -1).astype(jnp.bfloat16)
    )
    expert_part = jnp.dot(hidden, quantized, preferred_element_type=jnp.float32)
    expert_rows = lax.psum_scatter(
        expert_part.astype(jnp.bfloat16), "tensor", scatter_dimension=1, tiled=True
    )
    returned = lax.all_to_all(
        expert_rows.reshape(owners, capacity, -1), "dp", split_axis=0, concat_axis=0, tiled=True
    )
    moe = lax.dot_general(
        combine,
        returned.reshape(owners * capacity, -1),
        (((0,), (0,)), ((), ())),
        preferred_element_type=jnp.float32,
    )
    return (
        residual_out,
        moe.astype(jnp.bfloat16),
        quantized[None],
        gram.reshape(unit_count, PANEL)[None],
    )


def solution(mesh):
    placed = (
        P("dp", "tensor"),
        P("dp", "tensor", None),
        P("dp", None),
        P("tensor", None, None),
        P("tensor", "dp"),
        P("tensor"),
        P("dp", None),
        P("dp", None),
        P(),
        P("dp", "tensor", None),
        P("dp", "tensor", None),
        P("dp", "tensor", None),
        P("dp", "tensor", None),
    )
    return jax.shard_map(
        shards,
        mesh=mesh,
        in_specs=placed,
        out_specs=(
            P("dp", "tensor"),
            P("dp", "tensor"),
            P("dp", "tensor", None),
            P("dp", "tensor", None),
        ),
        check_vma=False,
    )
```

profile of v0, /device:TPU:8, one launch (start us, length us, event | category | flops | bytes accessed | tf_op | source)
XLA Modules:
  0.0 798.8 jit_solution(5185820478258272816)
XLA Ops:
  16.7 6.1 fusion.46
  22.8 6.7 copy_convert_fusion
  109.1 5.5 constant_dynamic-update-slice_fusion.1
  114.6 6.1 constant_dynamic-update-slice_fusion
  120.7 6.0 fusion.34
  126.7 7.2 slice_subtract_fusion
  184.1 5.3 constant_dynamic-update-slice_fusion.17
  189.4 7.1 constant_dynamic-update-slice_fusion.16
  196.5 6.4 fusion.32
  202.9 12.1 %slice_subtract_fusion.1 = f32[2,96,7168]{2,0,1:T(2,128)} fusion(f32[2,112,7168]{2,0,1:T(2,128)} %copy-done.4, f32[2,96,7168]{2,1,0:T(8,128)} %fusion.32), kind=kLoop, calls=%fused_computation.5 | loop fusion | flops 1376256 | bytes 16515072 | tf_op jit(solution)/shard_map/vmap()/sub | solution.py:45
  261.2 5.3 constant_dynamic-update-slice_fusion.33
  266.5 7.1 constant_dynamic-update-slice_fusion.32
  277.6 6.7 slice_subtract_fusion.2
  335.4 5.2 constant_dynamic-update-slice_fusion.50
  340.7 5.5 constant_dynamic-update-slice_fusion.49
  346.4 6.1 constant_dynamic-update-slice_fusion.48
  412.0 5.3 constant_dynamic-update-slice_fusion.65
  417.4 6.5 constant_dynamic-update-slice_fusion.64
  481.8 5.5 constant_dynamic-update-slice_fusion.81
  487.4 6.1 constant_dynamic-update-slice_fusion.80
  556.2 5.7 constant_dynamic-update-slice_fusion.98
  561.9 6.8 constant_dynamic-update-slice_fusion.97
  568.9 6.7 constant_dynamic-update-slice_fusion.96
  635.6 14.8 %convolution_convert_fusion = bf16[128,7168]{1,0:T(8,128)(2,1)} fusion(bf16[128,2048]{0,1:T(8,128)(2,1)S(1)} %bitcast.5494, bf16[2048,7168]{1,0:T(8,128)(2,1)} %all-gather.2.cloned.1.call-done), kind=kOutput, calls=%fused_computation.2 | convolution fusion | flops 3759013888 | bytes 31719424 | tf_op jit(solution)/shard_map/dot_general | solution.py:84
  655.8 5.7 constant_dynamic-update-slice_fusion.114
  661.6 28.9 %reduce-scatter.5.cloned.1.call-done = bf16[128,1792]{1,0:T(8,128)(2,1)} async-done(((bf16[128,7168]{1,0:T(8,128)(2,1)}), bf16[128,1792]{1,0:T(8,128)(2,1)}) %reduce-scatter.5.cloned.1.call-update) | async-done | bytes 458768 | tf_op jit(solution)/shard_map/reduce_scatter | solution.py:89
  691.7 9.8 %psum.7 = f32[128]{0:T(128)S(1)} all-reduce(f32[128]{0:T(128)S(1)} %get-tuple-element.966), channel_id=1, replica_groups=mesh['dp'=8,'tensor'=4] {'tensor'}, use_global_device_ids=true, to_apply=%region_10.11 | all-reduce | flops 128 | bytes 1024 | tf_op jit(solution)/shard_map/psum | solution.py:94
  706.2 6.7 constant_dynamic-update-slice_fusion.113
  720.2 8.0 constant_dynamic-update-slice_fusion.112
  732.9 19.8 %reduce-scatter.7.cloned.1.call-done = bf16[64,256]{1,0:T(8,128)(2,1)} async-done(((bf16[64,1024]{1,0:T(8,128)(2,1)}), bf16[64,256]{1,0:T(8,128)(2,1)}) %reduce-scatter.7.cloned.1.call-update) | async-done | bytes 32784 | tf_op jit(solution)/shard_map/reduce_scatter | solution.py:126
  756.5 24.2 %reduce-scatter.11.cloned.1.call-done = bf16[64,1792]{1,0:T(8,128)(2,1)} async-done(((bf16[64,7168]{1,0:T(8,128)(2,1)}), bf16[64,1792]{1,0:T(8,128)(2,1)}) %reduce-scatter.11.cloned.1.call-update) | async-done | bytes 229392 | tf_op jit(solution)/shard_map/reduce_scatter | solution.py:147
  785.3 5.7 all-to-all-done.1
  (1063 shorter events, 508.9 us)
Async XLA Ops:
  7.2 628.2 %all-gather.2.cloned.1.call-start = ((), (), s32[]{:S(2)}) async-start(), calls=%async_computation.6 | async-start | bytes 33030144 | tf_op jit(solution)/shard_map/all_gather | solution.py:86
  7.9 682.5 %reduce-scatter.5.cloned.1.call-start = ((), (), s32[]{:S(2)}) async-start(), calls=%async_computation.7 | async-start | bytes 2293760 | tf_op jit(solution)/shard_map/reduce_scatter | solution.py:89
  134.0 55.4 %copy-start.4 = (f32[2,112,7168]{2,0,1:T(2,128)}, f32[2,112,7168]{2,0,1:T(2,128)S(1)}, u32[]{:S(2)}) copy-start(f32[2,112,7168]{2,0,1:T(2,128)S(1)} %slice_subtract_fusion) | copy-start | bytes 19267588
  277.6 36.1 %copy-start.308 = (f32[2]{0:T(128)S(1)}, f32[2]{0:T(128)}, u32[]{:S(2)}) copy-start(f32[2]{0:T(128)} %get-tuple-element.594) | copy-start | bytes 28
  277.6 36.1 %copy-start.309 = (f32[2]{0:T(128)S(1)}, f32[2]{0:T(128)}, u32[]{:S(2)}) copy-start(f32[2]{0:T(128)} %get-tuple-element.595) | copy-start | bytes 28
  277.6 36.1 %copy-start.310 = (f32[2]{0:T(128)S(1)}, f32[2]{0:T(128)}, u32[]{:S(2)}) copy-start(f32[2]{0:T(128)} %get-tuple-element.596) | copy-start | bytes 28
  277.6 36.1 %copy-start.311 = (f32[2]{0:T(128)S(1)}, f32[2]{0:T(128)}, u32[]{:S(2)}) copy-start(f32[2]{0:T(128)} %get-tuple-element.597) | copy-start | bytes 28
  277.6 36.1 %copy-start.339 = (f32[2]{0:T(128)S(1)}, f32[2]{0:T(128)}, u32[]{:S(2)}) copy-start(f32[2]{0:T(128)} %get-tuple-element.1358) | copy-start | bytes 28
  497.8 34.6 %copy-start.180 = (f32[2]{0:T(128)S(1)}, f32[2]{0:T(128)}, u32[]{:S(2)}) copy-start(f32[2]{0:T(128)} %get-tuple-element.223) | copy-start | bytes 28
  497.8 34.6 %copy-start.181 = (f32[2]{0:T(128)S(1)}, f32[2]{0:T(128)}, u32[]{:S(2)}) copy-start(f32[2]{0:T(128)} %get-tuple-element.224) | copy-start | bytes 28
  497.8 34.6 %copy-start.182 = (f32[2]{0:T(128)S(1)}, f32[2]{0:T(128)}, u32[]{:S(2)}) copy-start(f32[2]{0:T(128)} %get-tuple-element.225) | copy-start | bytes 28
  497.8 34.6 %copy-start.183 = (f32[2]{0:T(128)S(1)}, f32[2]{0:T(128)}, u32[]{:S(2)}) copy-start(f32[2]{0:T(128)} %get-tuple-element.226) | copy-start | bytes 28
  497.9 34.6 %copy-start.184 = (f32[2]{0:T(128)S(1)}, f32[2]{0:T(128)}, u32[]{:S(2)}) copy-start(f32[2]{0:T(128)} %get-tuple-element.227) | copy-start | bytes 28
  497.9 34.6 %copy-start.185 = (f32[2]{0:T(128)S(1)}, f32[2]{0:T(128)}, u32[]{:S(2)}) copy-start(f32[2]{0:T(128)} %get-tuple-element.228) | copy-start | bytes 28
  497.9 34.6 %copy-start.315 = (f32[2]{0:T(128)S(1)}, f32[2]{0:T(128)}, u32[]{:S(2)}) copy-start(f32[2]{0:T(128)} %get-tuple-element.1308) | copy-start | bytes 28
  497.9 36.2 %copy-start.344 = (f32[2]{0:T(128)S(1)}, f32[2]{0:T(128)}, u32[]{:S(2)}) copy-start(f32[2]{0:T(128)} %get-tuple-element.221) | copy-start | bytes 28
  497.9 36.2 %copy-start.345 = (f32[2]{0:T(128)S(1)}, f32[2]{0:T(128)}, u32[]{:S(2)}) copy-start(f32[2]{0:T(128)} %get-tuple-element.222) | copy-start | bytes 28
  497.9 36.2 %copy-start.346 = (f32[2]{0:T(128)S(1)}, f32[2]{0:T(128)}, u32[]{:S(2)}) copy-start(f32[2]{0:T(128)} %get-tuple-element.216) | copy-start | bytes 28
  497.9 36.2 %copy-start.347 = (f32[2]{0:T(128)S(1)}, f32[2]{0:T(128)}, u32[]{:S(2)}) copy-start(f32[2]{0:T(128)} %get-tuple-element.217) | copy-start | bytes 28
  497.9 36.2 %copy-start.348 = (f32[2]{0:T(128)S(1)}, f32[2]{0:T(128)}, u32[]{:S(2)}) copy-start(f32[2]{0:T(128)} %get-tuple-element.218) | copy-start | bytes 28
  497.9 36.2 %copy-start.349 = (f32[2]{0:T(128)S(1)}, f32[2]{0:T(128)}, u32[]{:S(2)}) copy-start(f32[2]{0:T(128)} %get-tuple-element.219) | copy-start | bytes 28
  579.9 34.4 %copy-start.146 = (f32[2]{0:T(128)S(1)}, f32[2]{0:T(128)}, u32[]{:S(2)}) copy-start(f32[2]{0:T(128)} %get-tuple-element.112) | copy-start | bytes 28
  579.9 34.4 %copy-start.324 = (f32[2]{0:T(128)S(1)}, f32[2]{0:T(128)}, u32[]{:S(2)}) copy-start(f32[2]{0:T(128)} %get-tuple-element.1294) | copy-start | bytes 28
  650.4 40.0 %copy-start.11 = (bf16[128,1792]{1,0:T(8,128)(2,1)S(1)}, bf16[128,1792]{1,0:T(8,128)(2,1)}, u32[]{:S(2)}) copy-start(bf16[128,1792]{1,0:T(8,128)(2,1)} %param.13) | copy-start | bytes 1376260
  650.4 55.8 %copy-start.59 = (f32[2]{0:T(128)S(1)}, f32[2]{0:T(128)}, u32[]{:S(2)}) copy-start(f32[2]{0:T(128)} %get-tuple-element.1285) | copy-start | bytes 28
  702.5 10.4 %all-to-all-start = ((bf16[8,8,1792]{2,1,0:T(8,128)(2,1)}), bf16[8,8,1792]{2,1,0:T(8,128)(2,1)S(1)}, u32[]{:S(2)}, u32[]{:S(2)}) async-start(bf16[8,8,1792]{2,1,0:T(8,128)(2,1)} %fusion.5), calls=%async_computation.1 | async-start | bytes 458752 | tf_op jit(solution)/shard_map/all_to_all | solution.py:121
  706.1 26.8 %reduce-scatter.9.cloned.1.call-start = ((), (), s32[]{:S(2)}) async-start(), calls=%async_computation.9 | async-start | bytes 163840 | tf_op jit(solution)/shard_map/reduce_scatter | solution.py:129
  716.4 36.3 %reduce-scatter.7.cloned.1.call-start = ((), (), s32[]{:S(2)}) async-start(), calls=%async_computation.8 | async-start | bytes 163840 | tf_op jit(solution)/shard_map/reduce_scatter | solution.py:126
  720.0 60.8 %reduce-scatter.11.cloned.1.call-start = ((), (), s32[]{:S(2)}) async-start(), calls=%async_computation.10 | async-start | bytes 1146880 | tf_op jit(solution)/shard_map/reduce_scatter | solution.py:147
  728.2 63.8 %copy-start.1 = (bf16[128,16,192]{0,2,1:T(8,128)(2,1)S(1)}, bf16[128,16,192]{0,2,1:T(8,128)(2,1)}, u32[]{:S(2)}) copy-start(bf16[128,16,192]{0,2,1:T(8,128)(2,1)} %param.14) | copy-start | bytes 2359300
  732.9 51.5 %copy-start.17 = (bf16[64,256]{1,0:T(8,128)(2,1)S(1)}, bf16[64,256]{1,0:T(8,128)(2,1)}, u32[]{:S(2)}) copy-start(bf16[64,256]{1,0:T(8,128)(2,1)} %reduce-scatter.9.cloned.1.call-done) | copy-start | bytes 98308
  780.7 10.2 %all-to-all-start.1 = ((bf16[8,8,1792]{2,1,0:T(8,128)(2,1)}), bf16[8,8,1792]{2,1,0:T(8,128)(2,1)S(1)}, u32[]{:S(2)}, u32[]{:S(2)}) async-start(bf16[8,8,1792]{2,1,0:T(8,128)(2,1)} %bitcast.5497), calls=%async_computation.5 | async-start | bytes 458752 | tf_op jit(solution)/shard_map/all_to_all | solution.py:150
  (343 other events, 8440.2 us)
Sparse Core Ops, SparseCore 0:
  9.9 143.3 all-gather.1
  650.6 39.8 reduce-scatter.4
  716.5 15.9 reduce-scatter.8
  735.3 17.3 reduce-scatter.6
  756.6 24.0 reduce-scatter.10
where the time goes:
time: 812 us; the launch traced here: 799 us
  other arithmetic  568 us (70%)
  waiting for transfers between devices  79.3 us (10%)
  matrix products  64.8 us (8%)
  local copies, waits for them, and re-layouts  49.6 us (6%)
  between operations  19.3 us (2%)
  blocking collectives  9.75 us (1%)
    unnamed x217, other arithmetic  458 us
    another operation x7, other arithmetic, quantize_panel(): jnp.stack(errors)  45.8 us
    sub x7, other arithmetic, quantize_panel(): remaining - jnp.dot(coupling.T, jnp.stack(errors), precision=lax.Precisio...  35.4 us
    slice x53, local copies, waits for them, and re-layouts, quantize_panel(): current[later] = current[later] - strict[column, begin + later] * error  30.6 us
    reduce_scatter x1, waiting for transfers between devices, shards(): lax.psum_scatter(partial_out.astype(jnp.bfloat16), 'tensor', scatter_dime...  28.9 us
    dot_general x7, matrix products, quantize_panel(): jnp.dot(coupling.T, jnp.stack(errors), precision=lax.Precision.HIGHEST)  26.6 us
    reduce_scatter x1, waiting for transfers between devices, shards(): lax.psum_scatter(expert_part.astype(jnp.bfloat16), 'tensor', scatter_dime...  24.2 us
    reduce_scatter x1, waiting for transfers between devices, shards(): lax.psum_scatter(gate_part.astype(jnp.bfloat16), 'tensor', scatter_dimens...  19.8 us
  transfers between devices with their start and end apart: 7, of which 4 were waited for; matrix products, arithmetic and copies ran while one was open for 82% of the time, Pallas kernels for 0%

commit v1 on v0

v1 whole, which is shorter than its diff:
```python
import math

import jax
import jax.numpy as jnp
import numpy as np
from jax import lax
from jax.experimental import pallas as pl
from jax.experimental.pallas import tpu as pltpu
from jax.sharding import PartitionSpec as P

PANEL = 128
BLK = 16
LANES = 128
SUBS = 8
CAP = 8
ROUNDER = 12582912.0
VMEM_LIMIT = 60 * 2**20


def wave_coefficients():
    nodes = 0.5 * np.cos(np.pi * (np.arange(400) + 0.5) / 800)
    values = nodes - np.sin(2 * np.pi * nodes) / (2 * np.pi)
    basis = np.stack([nodes ** (2 * power + 1) for power in range(6)], axis=1)
    return [float(c) for c in np.linalg.lstsq(basis, values, rcond=None)[0]]


WAVE = wave_coefficients()


def split_bf16(x):
    first = x.astype(jnp.bfloat16)
    rest = x - first.astype(jnp.float32)
    second = rest.astype(jnp.bfloat16)
    third = (rest - second.astype(jnp.float32)).astype(jnp.bfloat16)
    return first, second, third


def quantize_kernel(top, held, scalars, factor, source, *rest):
    done = rest[:held]
    out, weight, nat, rows, errs, levs, levels, lows, steps, scales, in_sem, out_sem, done_sem, bounce = rest[-14:]
    columns = nat.shape[1]
    groups = columns // (SUBS * LANES)
    width = groups * SUBS
    blocks = PANEL // BLK

    def fetch(c):
        lanes = pl.ds(c * SUBS * LANES, SUBS * LANES)
        return pltpu.make_async_copy(
            source.at[pl.ds(top, PANEL), lanes], weight.at[:, lanes], in_sem.at[c]
        )

    for c in range(groups):
        fetch(c).start()
    carried = [pltpu.make_async_copy(ref, bounce, done_sem) for ref in done]
    for copy in carried:
        copy.start()
    for c in range(groups):
        fetch(c).wait()
        low, high = [], []
        for s in range(SUBS):
            lanes = pl.ds((c * SUBS + s) * LANES, LANES)
            block = weight[:, lanes].astype(jnp.float32)
            nat[:, lanes] = block
            low.append(jnp.min(block, axis=0, keepdims=True))
            high.append(jnp.max(block, axis=0, keepdims=True))
        low = jnp.concatenate(low, axis=0)
        high = jnp.concatenate(high, axis=0)
        step = (high - low) / 15.0 + 1e-05
        spot = pl.ds(c * SUBS, SUBS)
        lows[spot, :] = low
        steps[spot, :] = step
        scales[spot, :] = 1.0 / step

    def block_step(b, first_row):
        base = pl.multiple_of(b * BLK, BLK)
        for g in range(width):
            rows[pl.ds(g, BLK, stride=width), :] = nat[
                pl.ds(base, BLK), g * LANES : (g + 1) * LANES
            ]
        for k in range(BLK):
            here = pl.ds(k * width, width)
            current = rows[here, :]
            for i in range(k):
                current = current - scalars[base + i, base + k] * errs[pl.ds(i * width, width), :]
            low = lows[...]
            t = jnp.clip((current - low) * scales[...], 0.0, 15.0)
            whole = (t + ROUNDER) - ROUNDER
            u = t - whole
            square = u * u
            fourth = square * square
            wave = (WAVE[0] + WAVE[1] * square) + fourth * (
                (WAVE[2] + WAVE[3] * square) + fourth * (WAVE[4] + WAVE[5] * square)
            )
            level = low + steps[...] * (whole + wave * u)
            errs[here, :] = current - level
            levs[here, :] = level
        column = lax.broadcasted_iota(jnp.int32, (BLK, PANEL), 1)
        coupling = jnp.where(column >= base + BLK, factor[pl.ds(base, BLK), :], 0.0)
        u1, u2, u3 = split_bf16(coupling)
        left = jnp.concatenate([u1, u1, u1, u2, u2, u3], axis=0)[:, first_row:]
        for c in range(groups):

            def natural(ref):
                pieces = [
                    ref[pl.ds(c * SUBS + s, BLK, stride=width), :] for s in range(SUBS)
                ]
                return jnp.concatenate(pieces, axis=1)

            span = slice(c * SUBS * LANES, (c + 1) * SUBS * LANES)
            levels[pl.ds(base, BLK), span] = natural(levs).astype(levels.dtype)
            e1, e2, e3 = split_bf16(natural(errs))
            right = jnp.concatenate([e1, e2, e3, e1, e2, e1], axis=0)
            update = lax.dot_general(
                left, right, (((0,), (0,)), ((), ())), preferred_element_type=jnp.float32
            )
            nat[first_row:, span] = nat[first_row:, span] - update

    for begin in range(0, blocks, 2):

        def body(b, carry):
            block_step(b, (begin + 1) * BLK)
            return carry

        lax.fori_loop(begin, begin + 2, body, 0)
    store = pltpu.make_async_copy(levels, out.at[pl.ds(top, PANEL), :], out_sem)
    store.start()
    for copy in carried:
        copy.wait()
        back = pltpu.make_async_copy(bounce, out.at[pl.ds(0, top), :], done_sem)
        back.start()
        back.wait()
    store.wait()


def quantize_panel(index, factor, weight, partly, *after):
    columns = weight.shape[1]
    width = columns // LANES
    wide = pltpu.VMEM((BLK * width, LANES), jnp.float32)
    small = pltpu.VMEM((width, LANES), jnp.float32)
    anywhere = pl.BlockSpec(memory_space=pl.ANY)
    return pl.pallas_call(
        lambda *refs: quantize_kernel(index * PANEL, len(partly), *refs),
        out_shape=jax.ShapeDtypeStruct(((index + 1) * PANEL, columns), jnp.bfloat16),
        in_specs=[
            pl.BlockSpec(memory_space=pltpu.SMEM),
            pl.BlockSpec(memory_space=pltpu.VMEM),
            anywhere,
        ]
        + [anywhere] * (len(partly) + len(after)),
        out_specs=anywhere,
        scratch_shapes=[
            pltpu.VMEM((PANEL, columns), jnp.bfloat16),
            pltpu.VMEM((PANEL, columns), jnp.float32),
            wide,
            wide,
            wide,
            pltpu.VMEM((PANEL, columns), jnp.bfloat16),
            small,
            small,
            small,
            pltpu.SemaphoreType.DMA((columns // (SUBS * LANES),)),
            pltpu.SemaphoreType.DMA,
            pltpu.SemaphoreType.DMA,
            pltpu.VMEM((max(1, index) * PANEL, columns), jnp.bfloat16),
        ],
        compiler_params=pltpu.CompilerParams(vmem_limit_bytes=VMEM_LIMIT),
        cost_estimate=pl.CostEstimate(
            flops=16 * 10**9, bytes_accessed=4 * PANEL * columns, transcendentals=0
        ),
    )(factor, factor, weight, *partly, *after)


def scaled_factors(upper):
    blocks = upper.reshape(-1, PANEL, PANEL)
    index = jnp.arange(PANEL)
    diagonal = jnp.sum(
        jnp.where(index[:, None] == index[None, :], blocks, 0.0), axis=2, keepdims=True
    )
    return jnp.where(index[:, None] < index[None, :], blocks / diagonal, 0.0)


def project_kernel(arrays, core, own, partner, *rest):
    rows = rest[:arrays]
    outs = rest[-arrays - 6 : -6]
    columns, left, low, high, column_sem, row_sem = rest[-6:]
    tiles = column_sem.shape[1]
    tile = columns.shape[1] // tiles
    copies = []
    for k in range(tiles):
        span = pl.ds(k * tile, tile)
        for source, turn in ((own, core[0]), (partner, 1 - core[0])):
            copies.append(
                pltpu.make_async_copy(
                    source.at[span, :],
                    columns.at[turn, span, :],
                    column_sem.at[len(copies) % 2, k],
                )
            )
    joined = len(rows[0].shape) == 3
    gathers = [
        pltpu.make_async_copy(ref, left if joined else left.at[g], row_sem.at[g])
        for g, ref in enumerate(rows)
    ]
    for copy in gathers + copies:
        copy.start()
    for copy in gathers:
        copy.wait()
    for k in range(tiles):
        copies[2 * k].wait()
        copies[2 * k + 1].wait()
        span = slice(k * tile, (k + 1) * tile)
        part = left[:, :, span].reshape(-1, tile)
        for half, total in enumerate((low, high)):
            product = jnp.dot(part, columns[half, span, :], preferred_element_type=jnp.float32)
            total[...] = product if k == 0 else total[...] + product
    count = left.shape[1]
    width = own.shape[1]
    for g in range(left.shape[0]):
        out = outs[0].at[g] if joined else outs[g]
        span = slice(g * count, (g + 1) * count)
        out[:, :width] = low[span, :].astype(jnp.bfloat16)
        out[:, width:] = high[span, :].astype(jnp.bfloat16)


def project(core, rows, own, partner, *after):
    joined = rows[0].ndim == 3
    groups = rows[0].shape[0] if joined else len(rows)
    count, depth = rows[0].shape[-2:]
    width = own.shape[1]
    shape = (groups,) * joined + (count, 2 * width)
    tiles = depth // 512
    total = groups * count
    vmem = pl.BlockSpec(memory_space=pltpu.VMEM)
    anywhere = pl.BlockSpec(memory_space=pl.ANY)
    return pl.pallas_call(
        lambda *refs: project_kernel(len(rows), *refs),
        out_shape=[jax.ShapeDtypeStruct(shape, jnp.bfloat16)] * len(rows),
        in_specs=[pl.BlockSpec(memory_space=pltpu.SMEM)]
        + [anywhere] * (2 + len(rows) + len(after)),
        out_specs=[vmem] * len(rows),
        scratch_shapes=[
            pltpu.VMEM((2, depth, width), jnp.bfloat16),
            pltpu.VMEM((groups, count, depth), jnp.bfloat16),
            pltpu.VMEM((total, width), jnp.float32),
            pltpu.VMEM((total, width), jnp.float32),
            pltpu.SemaphoreType.DMA((2, tiles)),
            pltpu.SemaphoreType.DMA((groups,)),
        ],
        compiler_params=pltpu.CompilerParams(vmem_limit_bytes=VMEM_LIMIT),
        cost_estimate=pl.CostEstimate(
            flops=4 * total * depth * width,
            bytes_accessed=2 * (total * depth + 2 * depth * width + 2 * total * width),
            transcendentals=0,
        ),
    )(core, own, partner, *rows, *after)


def front_kernel(arrived, order, residual, pick, *rest):
    front, outgoing = rest[-2:]
    ranks, per, _, width = arrived.shape
    base = jnp.dot(order[...], residual[...], preferred_element_type=jnp.float32)
    for block in range(per):
        span = slice(block * width, (block + 1) * width)
        total = sum(arrived[rank, block].astype(jnp.float32) for rank in range(ranks))
        front[:, span] = (base[:, span] + total).astype(front.dtype)
    outgoing[...] = jnp.dot(
        pick[...], front[...], preferred_element_type=jnp.float32
    ).astype(outgoing.dtype)


def make_front(arrived, order, residual, pick, *after):
    columns = residual.shape[1]
    vmem = pl.BlockSpec(memory_space=pltpu.VMEM)
    return pl.pallas_call(
        front_kernel,
        out_shape=[
            jax.ShapeDtypeStruct((order.shape[0], columns), jnp.bfloat16),
            jax.ShapeDtypeStruct((pick.shape[0], columns), jnp.bfloat16),
        ],
        in_specs=[vmem] * 4 + [pl.BlockSpec(memory_space=pl.ANY)] * len(after),
        out_specs=[vmem, vmem],
        compiler_params=pltpu.CompilerParams(vmem_limit_bytes=VMEM_LIMIT),
        cost_estimate=pl.CostEstimate(
            flops=10**8, bytes_accessed=2 * arrived.size, transcendentals=0
        ),
    )(arrived, order, residual, pick, *after)


def gate_kernel(rows, gain, gate_w, up_w, *rest):
    packed, weights, gate, up, scaled, sem = rest[-6:]
    tiles = sem.shape[1]
    tile = weights.shape[1] // tiles
    copies = []
    for k in range(tiles):
        span = pl.ds(k * tile, tile)
        for which, source in enumerate((gate_w, up_w)):
            copies.append(
                pltpu.make_async_copy(
                    source.at[span, :], weights.at[which, span, :], sem.at[which, k]
                )
            )
    for copy in copies:
        copy.start()
    wide = rows[...].astype(jnp.float32)
    squares = jnp.sum(wide * wide, axis=1, keepdims=True)
    scaled[...] = (wide * gain[...].astype(jnp.float32)).astype(jnp.bfloat16)
    for k in range(tiles):
        span = slice(k * tile, (k + 1) * tile)
        for which, total in enumerate((gate, up)):
            copies[2 * k + which].wait()
            product = jnp.dot(
                scaled[:, span], weights[which, span, :], preferred_element_type=jnp.float32
            )
            total[...] = product if k == 0 else total[...] + product
    high = squares.astype(jnp.bfloat16).astype(jnp.float32)
    lane = lax.broadcasted_iota(jnp.int32, (rows.shape[0], LANES), 1)
    tail = jnp.where(lane == 0, high, jnp.where(lane == 1, squares - high, 0.0))
    ranks, _, width = packed.shape
    units = (width - LANES) // 2
    for rank in range(ranks):
        span = slice(rank * units, (rank + 1) * units)
        packed[rank, :, :units] = gate[:, span].astype(packed.dtype)
        packed[rank, :, units : 2 * units] = up[:, span].astype(packed.dtype)
        packed[rank, :, 2 * units :] = tail.astype(packed.dtype)


def gate_and_up(rows, gain, gate_w, up_w, ranks, *after):
    count, columns = rows.shape
    hidden = gate_w.shape[1]
    tiles = 7
    shape = (ranks, count, 2 * hidden // ranks + LANES)
    vmem = pl.BlockSpec(memory_space=pltpu.VMEM)
    anywhere = pl.BlockSpec(memory_space=pl.ANY)
    return pl.pallas_call(
        gate_kernel,
        out_shape=jax.ShapeDtypeStruct(shape, jnp.bfloat16),
        in_specs=[vmem, vmem, anywhere, anywhere] + [anywhere] * len(after),
        out_specs=vmem,
        scratch_shapes=[
            pltpu.VMEM((2, columns, hidden), jnp.bfloat16),
            pltpu.VMEM((count, hidden), jnp.float32),
            pltpu.VMEM((count, hidden), jnp.float32),
            pltpu.VMEM((count, columns), jnp.bfloat16),
            pltpu.SemaphoreType.DMA((2, tiles)),
        ],
        compiler_params=pltpu.CompilerParams(vmem_limit_bytes=VMEM_LIMIT),
        cost_estimate=pl.CostEstimate(
            flops=4 * count * columns * hidden,
            bytes_accessed=4 * columns * hidden,
            transcendentals=0,
        ),
    )(rows, gain, gate_w, up_w, *after)


def expert_kernel(model_width, packed, levels, *rest):
    out, gram, held, sem = rest[-4:]
    ranks, count, width = packed.shape
    units = (width - LANES) // 2
    tiles = sem.shape[0]
    tile = held.shape[1] // tiles
    copies = []
    for k in range(tiles):
        span = pl.ds(k * tile, tile)
        copies.append(pltpu.make_async_copy(levels.at[:, span], held.at[:, span], sem.at[k]))
    for copy in copies:
        copy.start()
    summed = sum(packed[rank].astype(jnp.float32) for rank in range(ranks))
    tail = summed[:, 2 * units :]
    lane = lax.broadcasted_iota(jnp.int32, tail.shape, 1)
    squares = jnp.sum(jnp.where(lane < 2, tail, 0.0), axis=1, keepdims=True)
    inverse = lax.rsqrt(squares / model_width + 1e-06)
    gate = summed[:, :units] * inverse
    up = summed[:, units : 2 * units] * inverse
    active = (gate / (1.0 + jnp.exp(-gate)) * up).astype(jnp.bfloat16)
    for panel in range(units // PANEL):
        span = slice(panel * PANEL, (panel + 1) * PANEL)
        gram[span, :] = (
            lax.dot_general(
                active[:, span],
                active[:, span],
                (((0,), (0,)), ((), ())),
                preferred_element_type=jnp.float32,
            )
            / count
        )
    for k in range(tiles):
        span = slice(k * tile, (k + 1) * tile)
        copies[k].wait()
        out[:, span] = jnp.dot(
            active, held[:, span], preferred_element_type=jnp.float32
        ).astype(out.dtype)


def expert_outputs(packed, levels, model_width, *after):
    ranks, count, width = packed.shape
    units, columns = levels.shape
    vmem = pl.BlockSpec(memory_space=pltpu.VMEM)
    anywhere = pl.BlockSpec(memory_space=pl.ANY)
    return pl.pallas_call(
        lambda *refs: expert_kernel(model_width, *refs),
        out_shape=[
            jax.ShapeDtypeStruct((count, columns), jnp.bfloat16),
            jax.ShapeDtypeStruct((units, PANEL), jnp.float32),
        ],
        in_specs=[vmem, anywhere] + [anywhere] * len(after),
        out_specs=[vmem, vmem],
        scratch_shapes=[
            pltpu.VMEM((units, columns), jnp.bfloat16),
            pltpu.SemaphoreType.DMA((7,)),
        ],
        compiler_params=pltpu.CompilerParams(vmem_limit_bytes=VMEM_LIMIT),
        cost_estimate=pl.CostEstimate(
            flops=2 * count * units * columns,
            bytes_accessed=2 * units * columns,
            transcendentals=count * units,
        ),
    )(packed, levels, *after)


def route_kernel(owners, ids, gates, table, order, pick, combine):
    picks, tokens = ids.shape
    first = pick.shape[1]
    experts = table.shape[1]
    kept = lax.broadcasted_iota(jnp.int32, (owners, experts), 0)
    number = lax.broadcasted_iota(jnp.int32, (owners, experts), 1)
    expert_of = jnp.sum(jnp.where(table[...] == kept, number, 0), axis=1, keepdims=True)
    hit = jnp.zeros((owners, tokens), jnp.float32)
    weight = jnp.zeros((owners, tokens), jnp.float32)
    for k in range(picks):
        match = ids[k : k + 1, :] == expert_of
        hit = jnp.where(match, 1.0, hit)
        weight = jnp.where(match, gates[k : k + 1, :].astype(jnp.float32) / 256.0, weight)
    picked = jnp.max(hit, axis=0, keepdims=True)
    row = lax.broadcasted_iota(jnp.int32, (tokens, tokens), 0)
    column = lax.broadcasted_iota(jnp.int32, (tokens, tokens), 1)
    earlier = (row < column).astype(jnp.float32).astype(jnp.bfloat16)

    def before(flags):
        wide = jnp.broadcast_to(flags, (max(8, flags.shape[0]), tokens)).astype(jnp.bfloat16)
        return jnp.dot(wide, earlier, preferred_element_type=jnp.float32)[: flags.shape[0]]

    ahead = before(picked)
    token = lax.broadcasted_iota(jnp.int32, (1, tokens), 1).astype(jnp.float32)
    count = jnp.sum(picked, axis=1, keepdims=True)
    place = jnp.where(picked > 0.0, ahead, count + token - ahead).astype(jnp.int32)
    moved = (row == place).astype(jnp.float32)
    order[...] = moved.astype(jnp.bfloat16)
    position = before(hit)
    spot = lax.broadcasted_iota(jnp.int32, (CAP, tokens), 0).astype(jnp.float32)
    chosen_rows, weighted = [], []
    for s in range(owners):
        select = jnp.where(position[s : s + 1] == spot, hit[s : s + 1], 0.0)
        chosen_rows.append(select)
        weighted.append(select * weight[s : s + 1])
    combine[...] = jnp.concatenate(weighted, axis=0).astype(jnp.bfloat16)
    pick[...] = lax.dot_general(
        jnp.concatenate(chosen_rows, axis=0).astype(jnp.bfloat16),
        moved[:first].astype(jnp.bfloat16),
        (((1,), (1,)), ((), ())),
        preferred_element_type=jnp.float32,
    ).astype(jnp.bfloat16)


def route(expert_ids, gate_num, slot_table, owners, first):
    tokens = expert_ids.shape[0]
    slots = owners * CAP
    return pl.pallas_call(
        lambda *refs: route_kernel(owners, *refs),
        out_shape=[
            jax.ShapeDtypeStruct((tokens, tokens), jnp.bfloat16),
            jax.ShapeDtypeStruct((slots, first), jnp.bfloat16),
            jax.ShapeDtypeStruct((slots, tokens), jnp.bfloat16),
        ],
        cost_estimate=pl.CostEstimate(flops=10**7, bytes_accessed=10**5, transcendentals=0),
    )(expert_ids.T, gate_num.T, slot_table[None, :])


NOPE = 128
ROPE = 64
VHEAD = 128
LATENT = 512


def attend(queries, latent, latent_up):
    seq_len, head_count = queries.shape[:2]
    scale = 1.0 / math.sqrt(NOPE + ROPE)
    key_value = jnp.einsum(
        "tc,hcd->thd", latent[:, :LATENT], latent_up, preferred_element_type=jnp.float32
    ).astype(jnp.bfloat16)
    rotary = jnp.broadcast_to(latent[:, None, LATENT:], (seq_len, head_count, ROPE))
    keys = jnp.concatenate([key_value[:, :, :NOPE], rotary], axis=2)
    scores = jnp.einsum("thd,shd->hts", queries, keys, preferred_element_type=jnp.float32) * scale
    causal = jnp.arange(seq_len)[None, :] <= jnp.arange(seq_len)[:, None]
    scores = jnp.where(causal[None], scores, -1e30)
    top = jnp.max(scores, axis=2, keepdims=True)
    expo = jnp.exp(scores - top)
    probs = (expo / jnp.sum(expo, axis=2, keepdims=True)).astype(jnp.bfloat16)
    result = jnp.einsum(
        "hts,shd->thd", probs, key_value[:, :, NOPE:], preferred_element_type=jnp.float32
    )
    return result.astype(jnp.bfloat16).reshape(seq_len, head_count * VHEAD)


def chosen(onehot, rows):
    return jnp.dot(onehot, rows, preferred_element_type=jnp.float32).astype(jnp.bfloat16)


def same_cores(chips):
    return [[2 * chip + core for chip in range(chips)] for core in range(2)]


def across_chips(chunks):
    groups = same_cores(chunks.shape[0])
    return lax.all_to_all(
        chunks, "dp", split_axis=0, concat_axis=0, axis_index_groups=groups, tiled=True
    )


def to_other_chips(chunks):
    owners = 2 * len(chunks)
    moved = [chunks[0]]
    for turn in range(1, len(chunks)):
        pairs = [(place, place ^ (2 * turn)) for place in range(owners)]
        moved.append(lax.ppermute(chunks[turn], "dp", pairs))
    return moved


def to_other_ranks(chunks):
    ranks = len(chunks)
    stacked = jnp.stack(chunks)
    chip = lax.div(lax.axis_index("dp"), 2)
    rank = lax.axis_index("tensor")
    moved = []
    for shift in range(ranks):
        spot = jnp.bitwise_xor(chip, lax.rem(rank + shift, ranks))
        chunk = lax.dynamic_slice(
            stacked, (spot, 0, 0), (1,) + stacked.shape[1:], allow_negative_indices=False
        )[0]
        if shift:
            pairs = [(place, (place + shift) % ranks) for place in range(ranks)]
            chunk = lax.ppermute(chunk, "tensor", pairs)
        moved.append(chunk)
    return moved


def across_ranks(chunks, ranks):
    chips, rows, width = chunks.shape
    chunks = chunks.reshape(ranks, chips // ranks, rows, width)
    return lax.all_to_all(chunks, "tensor", split_axis=0, concat_axis=0, tiled=True)


def shards(
    residual_in,
    queries,
    latent,
    latent_up,
    out_proj,
    norm_gain,
    expert_ids,
    gate_num,
    slot_table,
    gate_proj,
    up_proj,
    down_proj,
    inv_chol,
):
    seq_len, model_cols = residual_in.shape
    owners = lax.axis_size("dp")
    ranks = lax.axis_size("tensor")

    chips = owners // 2
    first = min(seq_len, owners * CAP) if chips == ranks == 4 else seq_len
    core = lax.rem(lax.axis_index("dp"), 2)[None]
    partner = lax.ppermute(out_proj, "dp", [(i, i ^ 1) for i in range(owners)])
    order_rows, pick, combine = route(expert_ids, gate_num, slot_table, owners, first)
    factors = scaled_factors(inv_chol[0])
    weight = down_proj[0]
    panels = factors.shape[0]
    attended = attend(queries, latent, latent_up)

    copies = chosen(jnp.tile(order_rows[:first], (chips, 1)), attended)
    everyone = across_chips(copies.reshape(chips, first, -1))
    later = []
    if first < seq_len and chips == ranks:
        later = to_other_chips([chosen(order_rows[first:], attended)] * chips)
    partly = [quantize_panel(0, factors[0], weight, [], copies, *later[:1])]
    chunks = project(core, [everyone], out_proj, partner, partly[0])[0]
    arrived = across_chips(chunks)
    for panel in range(1, panels):
        partly = [quantize_panel(panel, factors[panel], weight, partly, chunks)]
    if later:
        later = project(core, later, out_proj, partner, partly[0])
    quantized = partly[0]
    front, outgoing = make_front(
        across_ranks(arrived, ranks), order_rows[:first], residual_in, pick, quantized, *later
    )
    incoming = lax.all_to_all(
        outgoing.reshape(owners, CAP, -1), "dp", split_axis=0, concat_axis=0, tiled=True
    )
    if later:
        later = to_other_chips(later)
    packed = gate_and_up(
        incoming.reshape(owners * CAP, -1),
        norm_gain[None, :],
        gate_proj[0],
        up_proj[0],
        ranks,
        *later,
    )
    packed = lax.all_to_all(packed, "tensor", split_axis=0, concat_axis=0, tiled=True)
    if later:
        later = to_other_ranks(later)
    expert_part, gram = expert_outputs(packed, quantized, model_cols * ranks, *later)
    ordered_out = front
    if later:
        ordered_in = chosen(order_rows[first:], residual_in).astype(jnp.float32)
        back = ordered_in + sum(chunk.astype(jnp.float32) for chunk in later)
        ordered_out = jnp.concatenate([front, back.astype(jnp.bfloat16)], axis=0)
    residual_out = lax.dot_general(
        order_rows, ordered_out, (((0,), (0,)), ((), ())), preferred_element_type=jnp.float32
    ).astype(jnp.bfloat16)

    parcels = (
        expert_part.reshape(owners, CAP, ranks, model_cols)
        .swapaxes(1, 2)
        .reshape(owners * ranks, CAP, model_cols)
    )
    returned = lax.all_to_all(
        parcels, ("dp", "tensor"), split_axis=0, concat_axis=0, tiled=True
    ).reshape(owners * ranks * CAP, model_cols)
    weights = jnp.broadcast_to(
        combine.reshape(owners, 1, CAP, seq_len), (owners, ranks, CAP, seq_len)
    ).reshape(owners * ranks * CAP, seq_len)
    moe = lax.dot_general(
        weights, returned, (((0,), (0,)), ((), ())), preferred_element_type=jnp.float32
    )
    return (
        residual_out,
        moe.astype(jnp.bfloat16),
        quantized[None],
        gram[None],
    )


def solution(mesh):
    placed = (
        P("dp", "tensor"),
        P("dp", "tensor", None),
        P("dp", None),
        P("tensor", None, None),
        P("tensor", "dp"),
        P("tensor"),
        P("dp", None),
        P("dp", None),
        P(),
        P("dp", "tensor", None),
        P("dp", "tensor", None),
        P("dp", "tensor", None),
        P("dp", "tensor", None),
    )
    return jax.shard_map(
        shards,
        mesh=mesh,
        in_specs=placed,
        out_specs=(
            P("dp", "tensor"),
            P("dp", "tensor"),
            P("dp", "tensor", None),
            P("dp", "tensor", None),
        ),
        check_vma=False,
    )
```

time: 812 us -> 179 us (0.22); the launches traced: 799 us -> 177 us
  other arithmetic: 568 us -> 1.54 us
  Pallas kernels: 0 us -> 58.2 us
  matrix products: 64.8 us -> 13.1 us
  local copies, waits for them, and re-layouts: 49.6 us -> 7.97 us
  starting transfers between devices: 7.69 us -> 37 us
  waiting for transfers between devices: 79.3 us -> 58.6 us
  between operations: 19.3 us -> 1 us
  blocking collectives: 9.75 us -> 0 us
    unnamed x217 -> x0, other arithmetic: 458 us -> none
    reduce_scatter x4 -> x0, waiting for transfers between devices: 72.9 us -> none  [the longest x1 28.9 us: shards(): lax.psum_scatter(partial_out.astype(jnp.bfloat16), 'tensor', scatter_dime...]
    pallas_call x0 -> x8, Pallas kernels: none -> 58.2 us  [the longest x2 30.3 us: quantize_panel(): pl.pallas_call(lambda *refs: quantize_kernel(index * PANEL, len(partly),...]
    another operation x10 -> x1, other arithmetic: 56.4 us -> 1.27 us  [to_other_ranks(): stacked = jnp.stack(chunks)]
    dot_general x17 -> x8, matrix products: 63.7 us -> 12.5 us  [the longest x3 3.78 us: chosen(): jnp.dot(onehot, rows, preferred_element_type=jnp.float32)]
    sub x7 -> x0, other arithmetic: 35.4 us -> none  [quantize_panel(): remaining - jnp.dot(coupling.T, jnp.stack(errors), precision=lax.Precisio...]
    all_to_all x2 -> x6, waiting for transfers between devices: 5.68 us -> 35.9 us  [the longest x1 21.1 us: shards(): lax.all_to_all(parcels, ('dp', 'tensor'), split_axis=0, concat_axis=0, ti...]
    slice x58 -> x5, local copies, waits for them, and re-layouts: 31.1 us -> 0.93 us  [the longest x1 0.72 us: shards(): copies = chosen(jnp.tile(order_rows[:first], (chips, 1)), attended)]
  transfers between devices with their start and end apart: 7 -> 16, of which waited for: 4 -> 7; matrix products, arithmetic and copies ran while one was open for 82% -> 9% of each run, Pallas kernels for 0% -> 23%
where the time goes in v1:
time: 179 us; the launch traced here: 177 us
  waiting for transfers between devices  58.6 us (33%)
  Pallas kernels  58.2 us (33%)
  starting transfers between devices  37 us (21%)
  matrix products  13.1 us (7%)
  local copies, waits for them, and re-layouts  7.97 us (4%)
    pallas_call x2, Pallas kernels, quantize_panel(): pl.pallas_call(lambda *refs: quantize_kernel(index * PANEL, len(partly),...  30.3 us
    ppermute x3, waiting for transfers between devices, to_other_ranks(): chunk = lax.ppermute(chunk, 'tensor', pairs)  21.6 us
    all_to_all x1, waiting for transfers between devices, shards(): lax.all_to_all(parcels, ('dp', 'tensor'), split_axis=0, concat_axis=0, ti...  21.1 us
    pallas_call x2, Pallas kernels, project(): pl.pallas_call(lambda *refs: project_kernel(len(rows), *refs), out_shape=...  14 us
    all_to_all x2, waiting for transfers between devices, across_chips(): lax.all_to_all(chunks, 'dp', split_axis=0, concat_axis=0, axis_index_grou...  10.1 us
    all_to_all x2, starting transfers between devices, across_chips(): lax.all_to_all(chunks, 'dp', split_axis=0, concat_axis=0, axis_index_grou...  7.93 us
    ppermute x6, starting transfers between devices, to_other_chips(): moved.append(lax.ppermute(chunks[turn], 'dp', pairs))  7.16 us
    all_to_all x1, starting transfers between devices, across_ranks(): lax.all_to_all(chunks, 'tensor', split_axis=0, concat_axis=0, tiled=True)  5.33 us
  transfers between devices with their start and end apart: 16, of which 7 were waited for; matrix products, arithmetic and copies ran while one was open for 9% of the time, Pallas kernels for 23%

profile of v1, /device:TPU:8, one launch (start us, length us, event | category | flops | bytes accessed | tf_op | source)
XLA Modules:
  0.0 177.4 jit_solution(8845175160387354347)
XLA Ops:
  0.7 3.1 %convolution_convert_fusion.5 = bf16[128,16,256]{2,0,1:T(8,128)(2,1)S(1)} fusion(bf16[16,512,256]{2,1,0:T(8,128)(2,1)} %param.16, bf16[128,576]{0,1:T(8,128)(2,1)} %param.15), kind=kOutput, calls=%fused_computation.7 | convolution fusion | flops 537395200 | bytes 5373952 | tf_op jit(solution)/shard_map/tc,hcd->thd/dot_general | solution.py:487
  4.0 1.7 shard_map.156
  7.1 1.4 fusion.5
  8.5 2.1 %convolution_convert_fusion.6 = bf16[16,128,128]{2,1,0:T(8,128)(2,1)S(1)} fusion(bf16[128,16,256]{2,0,1:T(8,128)(2,1)S(1)} %convolution_convert_fusion.5, f32[16,128]{1,0:T(8,128)S(1)} %fusion.30, f32[16,128,128]{1,2,0:T(8,128)} %fusion.5), kind=kOutput, calls=%fused_computation.13 | convolution fusion | flops 68159616 | bytes 3153920 | tf_op jit(solution)/shard_map/hts,shd->thd/dot_general | solution.py:498
  10.6 1.4 convolution_convert_fusion.refs_3_
  12.1 3.7 %all-to-all-start = ((bf16[4,64,2048]{2,1,0:T(8,128)(2,1)}), bf16[4,64,2048]{2,1,0:T(8,128)(2,1)S(1)}, u32[]{:S(2)}, u32[]{:S(2)}) async-start(bf16[4,64,2048]{2,1,0:T(8,128)(2,1)} %bitcast.9), calls=%async_computation | async-start | bytes 2097152 | tf_op jit(solution)/shard_map/all_to_all | solution.py:514
  17.7 14.9 %shard_map.157.refs_4_.refs_3_ = bf16[128,7168]{1,0:T(8,128)(2,1)} custom-call(f32[128,128]{1,0:T(8,128)} %get-tuple-element.30.refs_0_.refs_1_, f32[128,128]{1,0:T(8,128)} %get-tuple-element.30.refs_0_.refs_1_, bf16[256,7168]{1,0:T(8,128)(2,1)} %bitcast.88, bf16[256,2048]{1,0:T(8,128)(2,1)} %convolution_convert_fusion.refs_3_, ...), custom_call_target="tpu_custom_call" | custom-call | flops 16000000000 | bytes 3670016 | tf_op jit(solution)/shard_map/pallas_call | solution.py:141
  33.6 7.1 %shard_map.158.refs_4_ = bf16[4,64,1792]{2,1,0:T(8,128)(2,1)} custom-call(s32[1]{0:T(128)} %bitcast.3.refs_0_, bf16[2048,896]{1,0:T(8,128)(2,1)} %refs_1_.3, bf16[2048,896]{1,0:T(8,128)(2,1)} %collective-permute-done.refs_2_, bf16[4,64,2048]{2,1,0:T(8,128)(2,1)} %copy-done.1, bf16[128,7168]{1,0:T(8,128)(2,1)} %shard_map.157.refs_4_.refs_3_), custom_call_target="tpu_custom_call" | custom-call | flops 1879048192 | bytes 9306112 | tf_op jit(solution)/shard_map/pallas_call | solution.py:235
  40.7 4.2 %all-to-all-start.1 = ((bf16[4,64,1792]{2,1,0:T(8,128)(2,1)}), bf16[4,64,1792]{2,1,0:T(8,128)(2,1)}, u32[]{:S(2)}, u32[]{:S(2)}) async-start(bf16[4,64,1792]{2,1,0:T(8,128)(2,1)} %shard_map.158.refs_4_), calls=%async_computation.1 | async-start | bytes 1835008 | tf_op jit(solution)/shard_map/all_to_all | solution.py:514
  44.9 2.1 %collective-permute-start.1 = (bf16[64,2048]{1,0:T(8,128)(2,1)S(1)}, bf16[64,2048]{1,0:T(8,128)(2,1)S(1)}, u32[]{:S(2)}, u32[]{:S(2)}) collective-permute-start(bf16[64,2048]{1,0:T(8,128)(2,1)S(1)} %copy-done.7), channel_id=1, source_target_pairs={{0,8},{4,12},{8,0},{12,4},{16,24},{20,28},{24,16},{28,20},{1,9},{5... | collective-permute-start | bytes 786440 | tf_op jit(solution)/shard_map/ppermute | solution.py:524
  47.0 1.5 collective-permute-start.2
  48.6 10.1 %all-to-all-done.1 = bf16[4,64,1792]{2,1,0:T(8,128)(2,1)} async-done(((bf16[4,64,1792]{2,1,0:T(8,128)(2,1)}), bf16[4,64,1792]{2,1,0:T(8,128)(2,1)}, u32[]{:S(2)}, u32[]{:S(2)}) %all-to-all-start.1) | async-done | bytes 917536 | tf_op jit(solution)/shard_map/all_to_all | solution.py:514
  58.6 5.3 %all-to-all-start.2 = ((bf16[4,1,64,1792]{3,2,1,0:T(8,128)(2,1)}), bf16[4,1,64,1792]{3,2,1,0:T(8,128)(2,1)S(1)}, u32[]{:S(2)}, u32[]{:S(2)}) async-start(bf16[4,1,64,1792]{3,2,1,0:T(8,128)(2,1)} %bitcast.16), calls=%async_computation.2 | async-start | bytes 1835008 | tf_op jit(solution)/shard_map/all_to_all | solution.py:549
  64.0 15.4 %shard_map.159.refs_7_.rest_0_.refs_1_ = bf16[256,7168]{1,0:T(8,128)(2,1)} custom-call(f32[128,128]{1,0:T(8,128)} %get-tuple-element.31.refs_0_.refs_1_, f32[128,128]{1,0:T(8,128)} %get-tuple-element.31.refs_0_.refs_1_, bf16[256,7168]{1,0:T(8,128)(2,1)} %bitcast.89, bf16[128,7168]{1,0:T(8,128)(2,1)} %shard_map.157.refs_4_.refs_3_, ...), custom_call_target="tpu_custom_call" | custom-call | flops 16000000000 | bytes 3670016 | tf_op jit(solution)/shard_map/pallas_call | solution.py:141
  80.9 7.0 %shard_map.160 = (bf16[64,1792]{1,0:T(8,128)(2,1)}, bf16[64,1792]{1,0:T(8,128)(2,1)}, bf16[64,1792]{1,0:T(8,128)(2,1)}, bf16[64,1792]{1,0:T(8,128)(2,1)}) custom-call(s32[1]{0:T(128)} %bitcast.3.refs_0_, bf16[2048,896]{1,0:T(8,128)(2,1)} %refs_1_.3, bf16[2048,896]{1,0:T(8,128)(2,1)} %collective-permute-done.refs_2_, ...), custom_call_target="tpu_custom_call" | custom-call | flops 1879048192 | bytes 9306112 | tf_op jit(solution)/shard_map/pallas_call | solution.py:235
  87.9 1.5 collective-permute-start.4
  90.0 1.5 collective-permute-start.6
  92.4 2.4 %shard_map.161 = (bf16[64,1792]{1,0:T(8,128)(2,1)}, bf16[64,1792]{1,0:T(8,128)(2,1)}) custom-call(bf16[4,1,64,1792]{3,2,1,0:T(8,128)(2,1)} %copy-done.2, bf16[64,128]{1,0:T(8,128)(2,1)} %copy-done.21, bf16[128,1792]{1,0:T(8,128)(2,1)} %residual.1, bf16[64,64]{1,0:T(8,128)(2,1)} %get-tuple-element.16.pick, ...), custom_call_target="tpu_custom_call" | custom-call | flops 100000000 | bytes 917504 | tf_op jit(solution)/shard_map/pallas_call | solution.py:274
  94.8 3.4 %all-to-all-start.3 = ((bf16[8,8,1792]{2,1,0:T(8,128)(2,1)}), bf16[8,8,1792]{2,1,0:T(8,128)(2,1)S(1)}, u32[]{:S(2)}, u32[]{:S(2)}) async-start(bf16[8,8,1792]{2,1,0:T(8,128)(2,1)} %bitcast.84), calls=%async_computation.3 | async-start | bytes 458752 | tf_op jit(solution)/shard_map/all_to_all | solution.py:597
  100.0 4.7 %all-to-all-done.3 = bf16[8,8,1792]{2,1,0:T(8,128)(2,1)S(1)} async-done(((bf16[8,8,1792]{2,1,0:T(8,128)(2,1)}), bf16[8,8,1792]{2,1,0:T(8,128)(2,1)S(1)}, u32[]{:S(2)}, u32[]{:S(2)}) %all-to-all-start.3) | async-done | bytes 229408 | tf_op jit(solution)/shard_map/all_to_all | solution.py:597
  105.4 5.2 %shard_map.162 = bf16[4,64,640]{2,1,0:T(8,128)(2,1)} custom-call(bf16[64,1792]{1,0:T(8,128)(2,1)} %bitcast.80, bf16[1,1792]{1,0:T(2,128)(2,1)} %broadcast_in_dim.78.gain, bf16[1792,1024]{1,0:T(8,128)(2,1)} %bitcast.71, bf16[1792,1024]{1,0:T(8,128)(2,1)} %bitcast.72, bf16[64,1792]{1,0:T(8,128)(2,1)} %get-tuple-element.17.rest_1_.rest_0_, ...), custom_call_target="tpu_custom_call" | custom-call | flops 469762048 | bytes 7340032 | tf_op jit(solution)/shard_map/pallas_call | solution.py:334
  110.6 5.1 %all-to-all-start.4 = ((bf16[4,64,640]{2,1,0:T(8,128)(2,1)}), bf16[4,64,640]{2,1,0:T(8,128)(2,1)S(1)}, u32[]{:S(2)}, u32[]{:S(2)}) async-start(bf16[4,64,640]{2,1,0:T(8,128)(2,1)} %shard_map.162), calls=%async_computation.4 | async-start | bytes 655360 | tf_op jit(solution)/shard_map/all_to_all | solution.py:610
  115.7 1.3 pad_maximum_fusion
  117.8 1.5 collective-permute-start.7
  120.1 2.0 %collective-permute-start.9 = (bf16[64,1792]{1,0:T(8,128)(2,1)S(1)}, bf16[64,1792]{1,0:T(8,128)(2,1)S(1)}, u32[]{:S(2)}, u32[]{:S(2)}) collective-permute-start(bf16[64,1792]{1,0:T(8,128)(2,1)S(1)} %get-tuple-element.27), channel_id=1, source_target_pairs={{0,3},{1,0},{2,1},{3,2},{4,7},{5,4},{6,5},{7,6},{8,11},{9,8},{10,9... | collective-permute-start | bytes 688136 | tf_op jit(solution)/shard_map/ppermute | solution.py:541
  122.2 15.6 %collective-permute-done.7.refs_3_ = bf16[64,1792]{1,0:T(8,128)(2,1)S(1)} collective-permute-done((bf16[64,1792]{1,0:T(8,128)(2,1)S(1)}, bf16[64,1792]{1,0:T(8,128)(2,1)S(1)}, u32[]{:S(2)}, u32[]{:S(2)}) %collective-permute-start.7) | collective-permute-done | bytes 229408 | tf_op jit(solution)/shard_map/ppermute | solution.py:541
  137.8 4.0 %collective-permute-done.8.refs_4_ = bf16[64,1792]{1,0:T(8,128)(2,1)S(1)} collective-permute-done((bf16[64,1792]{1,0:T(8,128)(2,1)S(1)}, bf16[64,1792]{1,0:T(8,128)(2,1)S(1)}, u32[]{:S(2)}, u32[]{:S(2)}) %collective-permute-start.8) | collective-permute-done | bytes 229408 | tf_op jit(solution)/shard_map/ppermute | solution.py:541
  141.8 1.9 %collective-permute-done.9.refs_5_ = bf16[64,1792]{1,0:T(8,128)(2,1)S(1)} collective-permute-done((bf16[64,1792]{1,0:T(8,128)(2,1)S(1)}, bf16[64,1792]{1,0:T(8,128)(2,1)S(1)}, u32[]{:S(2)}, u32[]{:S(2)}) %collective-permute-start.9) | collective-permute-done | bytes 229408 | tf_op jit(solution)/shard_map/ppermute | solution.py:541
  144.5 4.5 %shard_map.163 = (bf16[64,7168]{1,0:T(8,128)(2,1)}, f32[256,128]{1,0:T(8,128)}) custom-call(bf16[4,64,640]{2,1,0:T(8,128)(2,1)} %copy-done.6, bf16[256,7168]{1,0:T(8,128)(2,1)} %shard_map.159.refs_7_.rest_0_.refs_1_, bf16[64,1792]{1,0:T(8,128)(2,1)} %get-tuple-element.26.refs_2_, bf16[64,1792]{1,0:T(8,128)(2,1)} %copy-done.11, bf16[64,1792]{1,0:T(8,128)(2,1)} %copy-done.12, ...), custom_call_target="tpu_custom_call" | custom-call | flops 234881024 | bytes 3670016 | tf_op jit(solution)/shard_map/pallas_call | solution.py:399
  149.1 3.6 %all-to-all-start.5 = ((bf16[32,8,1792]{2,1,0:T(8,128)(2,1)}), bf16[32,8,1792]{2,1,0:T(8,128)(2,1)S(1)}, u32[]{:S(2)}, u32[]{:S(2)}) async-start(bf16[32,8,1792]{2,1,0:T(8,128)(2,1)} %bitcast.76), calls=%async_computation.5 | async-start | bytes 1835008 | tf_op jit(solution)/shard_map/all_to_all | solution.py:628
  152.7 1.4 add_convert_fusion
  155.2 21.1 %all-to-all-done.5 = bf16[32,8,1792]{2,1,0:T(8,128)(2,1)S(1)} async-done(((bf16[32,8,1792]{2,1,0:T(8,128)(2,1)}), bf16[32,8,1792]{2,1,0:T(8,128)(2,1)S(1)}, u32[]{:S(2)}, u32[]{:S(2)}) %all-to-all-start.5) | async-done | bytes 917536 | tf_op jit(solution)/shard_map/all_to_all | solution.py:628
  (83 shorter events, 14.7 us)
Async XLA Ops:
  0.6 5.9 %copy-start = (bf16[128,16,192]{0,2,1:T(8,128)(2,1)S(1)}, bf16[128,16,192]{0,2,1:T(8,128)(2,1)}, u32[]{:S(2)}) copy-start(bf16[128,16,192]{0,2,1:T(8,128)(2,1)} %param.14) | copy-start | bytes 2359300
  0.6 3.3 %slice-start = ((bf16[128,576]{0,1:T(8,128)(2,1)}), bf16[128,64]{0,1:T(8,128)(2,1)S(1)}, s32[]{:S(2)}) async-start(bf16[128,576]{0,1:T(8,128)(2,1)} %param.15), calls=%async_computation.6 | async-start | bytes 32768 | tf_op jit(solution)/shard_map/slice | solution.py:490
  0.7 32.0 %collective-permute-start = (bf16[2048,896]{1,0:T(8,128)(2,1)}, bf16[2048,896]{1,0:T(8,128)(2,1)}, u32[]{:S(2)}, u32[]{:S(2)}) collective-permute-start(bf16[2048,896]{1,0:T(8,128)(2,1)} %refs_1_.3), channel_id=1, source_target_pairs={{0,4},{4,0},{8,12},{12,8},{16,20},{20,16},{24,28},{28,24},{1,5},{5... | collective-permute-start | bytes 11010056 | tf_op jit(solution)/shard_map/ppermute | solution.py:574
  6.4 4.2 %copy-start.21 = (bf16[64,128]{1,0:T(8,128)(2,1)}, bf16[64,128]{1,0:T(8,128)(2,1)S(1)}, u32[]{:S(2)}) copy-start(bf16[64,128]{1,0:T(8,128)(2,1)S(1)} %slice.26.order) | copy-start | bytes 49156
  8.5 7.3 %copy-start.15 = (f32[1,256,128]{2,1,0:T(8,128)S(1)}, f32[1,256,128]{2,1,0:T(8,128)}, u32[]{:S(2)}) copy-start(f32[1,256,128]{2,1,0:T(8,128)} %param.25) | copy-start | bytes 393220
  8.5 8.2 %copy-start.20 = (bf16[128,128]{1,0:T(8,128)(2,1)S(1)}, bf16[128,128]{1,0:T(8,128)(2,1)}, u32[]{:S(2)}) copy-start(bf16[128,128]{1,0:T(8,128)(2,1)} %get-tuple-element.15) | copy-start | bytes 98308
  12.1 20.6 %all-to-all-start = ((bf16[4,64,2048]{2,1,0:T(8,128)(2,1)}), bf16[4,64,2048]{2,1,0:T(8,128)(2,1)S(1)}, u32[]{:S(2)}, u32[]{:S(2)}) async-start(bf16[4,64,2048]{2,1,0:T(8,128)(2,1)} %bitcast.9), calls=%async_computation | async-start | bytes 2097152 | tf_op jit(solution)/shard_map/all_to_all | solution.py:514
  33.6 11.3 %copy-start.7 = (bf16[64,2048]{1,0:T(8,128)(2,1)S(1)}, bf16[64,2048]{1,0:T(8,128)(2,1)}, u32[]{:S(2)}) copy-start(bf16[64,2048]{1,0:T(8,128)(2,1)} %convolution_convert_fusion.4.refs_4_.refs_3_) | copy-start | bytes 786436
  40.7 17.9 %all-to-all-start.1 = ((bf16[4,64,1792]{2,1,0:T(8,128)(2,1)}), bf16[4,64,1792]{2,1,0:T(8,128)(2,1)}, u32[]{:S(2)}, u32[]{:S(2)}) async-start(bf16[4,64,1792]{2,1,0:T(8,128)(2,1)} %shard_map.158.refs_4_), calls=%async_computation.1 | async-start | bytes 1835008 | tf_op jit(solution)/shard_map/all_to_all | solution.py:514
  44.9 34.5 %collective-permute-start.1 = (bf16[64,2048]{1,0:T(8,128)(2,1)S(1)}, bf16[64,2048]{1,0:T(8,128)(2,1)S(1)}, u32[]{:S(2)}, u32[]{:S(2)}) collective-permute-start(bf16[64,2048]{1,0:T(8,128)(2,1)S(1)} %copy-done.7), channel_id=1, source_target_pairs={{0,8},{4,12},{8,0},{12,4},{16,24},{20,28},{24,16},{28,20},{1,9},{5... | collective-permute-start | bytes 786440 | tf_op jit(solution)/shard_map/ppermute | solution.py:524
  47.0 32.4 %collective-permute-start.2 = (bf16[64,2048]{1,0:T(8,128)(2,1)S(1)}, bf16[64,2048]{1,0:T(8,128)(2,1)S(1)}, u32[]{:S(2)}, u32[]{:S(2)}) collective-permute-start(bf16[64,2048]{1,0:T(8,128)(2,1)S(1)} %copy-done.7), channel_id=1, source_target_pairs={{0,16},{4,20},{8,24},{12,28},{16,0},{20,4},{24,8},{28,12},{1,17},{... | collective-permute-start | bytes 786440 | tf_op jit(solution)/shard_map/ppermute | solution.py:524
  48.5 31.0 %collective-permute-start.3 = (bf16[64,2048]{1,0:T(8,128)(2,1)S(1)}, bf16[64,2048]{1,0:T(8,128)(2,1)S(1)}, u32[]{:S(2)}, u32[]{:S(2)}) collective-permute-start(bf16[64,2048]{1,0:T(8,128)(2,1)S(1)} %copy-done.7), channel_id=1, source_target_pairs={{0,24},{4,28},{8,16},{12,20},{16,8},{20,12},{24,0},{28,4},{1,25},{... | collective-permute-start | bytes 786440 | tf_op jit(solution)/shard_map/ppermute | solution.py:524
  58.6 32.8 %all-to-all-start.2 = ((bf16[4,1,64,1792]{3,2,1,0:T(8,128)(2,1)}), bf16[4,1,64,1792]{3,2,1,0:T(8,128)(2,1)S(1)}, u32[]{:S(2)}, u32[]{:S(2)}) async-start(bf16[4,1,64,1792]{3,2,1,0:T(8,128)(2,1)} %bitcast.16), calls=%async_computation.2 | async-start | bytes 1835008 | tf_op jit(solution)/shard_map/all_to_all | solution.py:549
  87.9 10.3 %copy-start.23 = (bf16[1792]{0:T(1024)(128)(2,1)S(1)}, bf16[1792]{0:T(1024)(128)(2,1)}, u32[]{:S(2)}) copy-start(bf16[1792]{0:T(1024)(128)(2,1)} %param.18) | copy-start | bytes 10756
  87.9 10.9 %collective-permute-start.4 = (bf16[64,1792]{1,0:T(8,128)(2,1)}, bf16[64,1792]{1,0:T(8,128)(2,1)S(1)}, u32[]{:S(2)}, u32[]{:S(2)}) collective-permute-start(bf16[64,1792]{1,0:T(8,128)(2,1)} %get-tuple-element.18.rest_2_), channel_id=1, source_target_pairs={{0,8},{4,12},{8,0},{12,4},{16,24},{20,28},{24,16},{28,20},{1,9},{5... | collective-permute-start | bytes 688136 | tf_op jit(solution)/shard_map/ppermute | solution.py:524
  89.5 10.5 %collective-permute-start.5 = (bf16[64,1792]{1,0:T(8,128)(2,1)}, bf16[64,1792]{1,0:T(8,128)(2,1)S(1)}, u32[]{:S(2)}, u32[]{:S(2)}) collective-permute-start(bf16[64,1792]{1,0:T(8,128)(2,1)} %get-tuple-element.19.rest_3_), channel_id=1, source_target_pairs={{0,16},{4,20},{8,24},{12,28},{16,0},{20,4},{24,8},{28,12},{1,17},{... | collective-permute-start | bytes 688136 | tf_op jit(solution)/shard_map/ppermute | solution.py:524
  90.0 10.0 %collective-permute-start.6 = (bf16[64,1792]{1,0:T(8,128)(2,1)}, bf16[64,1792]{1,0:T(8,128)(2,1)S(1)}, u32[]{:S(2)}, u32[]{:S(2)}) collective-permute-start(bf16[64,1792]{1,0:T(8,128)(2,1)} %get-tuple-element.20.rest_4_), channel_id=1, source_target_pairs={{0,24},{4,28},{8,16},{12,20},{16,8},{20,12},{24,0},{28,4},{1,25},{... | collective-permute-start | bytes 688136 | tf_op jit(solution)/shard_map/ppermute | solution.py:524
  94.8 9.9 %all-to-all-start.3 = ((bf16[8,8,1792]{2,1,0:T(8,128)(2,1)}), bf16[8,8,1792]{2,1,0:T(8,128)(2,1)S(1)}, u32[]{:S(2)}, u32[]{:S(2)}) async-start(bf16[8,8,1792]{2,1,0:T(8,128)(2,1)} %bitcast.84), calls=%async_computation.3 | async-start | bytes 458752 | tf_op jit(solution)/shard_map/all_to_all | solution.py:597
  98.8 5.9 %copy-start.8 = (bf16[64,1792]{1,0:T(8,128)(2,1)}, bf16[64,1792]{1,0:T(8,128)(2,1)S(1)}, u32[]{:S(2)}) copy-start(bf16[64,1792]{1,0:T(8,128)(2,1)S(1)} %collective-permute-done.4.rest_1_) | copy-start | bytes 688132
  100.0 4.8 %copy-start.9 = (bf16[64,1792]{1,0:T(8,128)(2,1)}, bf16[64,1792]{1,0:T(8,128)(2,1)S(1)}, u32[]{:S(2)}) copy-start(bf16[64,1792]{1,0:T(8,128)(2,1)S(1)} %collective-permute-done.5.rest_2_) | copy-start | bytes 688132
  100.0 4.7 %copy-start.10 = (bf16[64,1792]{1,0:T(8,128)(2,1)}, bf16[64,1792]{1,0:T(8,128)(2,1)S(1)}, u32[]{:S(2)}) copy-start(bf16[64,1792]{1,0:T(8,128)(2,1)S(1)} %collective-permute-done.6.rest_3_) | copy-start | bytes 688132
  105.4 10.3 %copy-start.3 = (bf16[64,1792]{1,0:T(8,128)(2,1)S(1)}, bf16[64,1792]{1,0:T(8,128)(2,1)}, u32[]{:S(2)}) copy-start(bf16[64,1792]{1,0:T(8,128)(2,1)} %get-tuple-element.17.rest_1_.rest_0_) | copy-start | bytes 688132
  110.6 33.1 %all-to-all-start.4 = ((bf16[4,64,640]{2,1,0:T(8,128)(2,1)}), bf16[4,64,640]{2,1,0:T(8,128)(2,1)S(1)}, u32[]{:S(2)}, u32[]{:S(2)}) async-start(bf16[4,64,640]{2,1,0:T(8,128)(2,1)} %shard_map.162), calls=%async_computation.4 | async-start | bytes 655360 | tf_op jit(solution)/shard_map/all_to_all | solution.py:610
  117.8 34.9 %copy-start.4 = (bf16[64,1792]{1,0:T(8,128)(2,1)S(1)}, bf16[64,1792]{1,0:T(8,128)(2,1)}, u32[]{:S(2)}) copy-start(bf16[64,1792]{1,0:T(8,128)(2,1)} %get-tuple-element.26.refs_2_) | copy-start | bytes 688132
  117.8 34.9 %copy-start.5 = (bf16[128,1792]{1,0:T(8,128)(2,1)S(1)}, bf16[128,1792]{1,0:T(8,128)(2,1)}, u32[]{:S(2)}) copy-start(bf16[128,1792]{1,0:T(8,128)(2,1)} %residual.1) | copy-start | bytes 1376260
  117.8 20.0 %collective-permute-start.7 = (bf16[64,1792]{1,0:T(8,128)(2,1)S(1)}, bf16[64,1792]{1,0:T(8,128)(2,1)S(1)}, u32[]{:S(2)}, u32[]{:S(2)}) collective-permute-start(bf16[64,1792]{1,0:T(8,128)(2,1)S(1)} %get-tuple-element.29), channel_id=1, source_target_pairs={{0,1},{1,2},{2,3},{3,0},{4,5},{5,6},{6,7},{7,4},{8,9},{9,10},{10,1... | collective-permute-start | bytes 688136 | tf_op jit(solution)/shard_map/ppermute | solution.py:541
  119.2 22.6 %collective-permute-start.8 = (bf16[64,1792]{1,0:T(8,128)(2,1)S(1)}, bf16[64,1792]{1,0:T(8,128)(2,1)S(1)}, u32[]{:S(2)}, u32[]{:S(2)}) collective-permute-start(bf16[64,1792]{1,0:T(8,128)(2,1)S(1)} %get-tuple-element.28), channel_id=1, source_target_pairs={{0,2},{1,3},{2,0},{3,1},{4,6},{5,7},{6,4},{7,5},{8,10},{9,11},{10,... | collective-permute-start | bytes 688136 | tf_op jit(solution)/shard_map/ppermute | solution.py:541
  120.1 23.6 %collective-permute-start.9 = (bf16[64,1792]{1,0:T(8,128)(2,1)S(1)}, bf16[64,1792]{1,0:T(8,128)(2,1)S(1)}, u32[]{:S(2)}, u32[]{:S(2)}) collective-permute-start(bf16[64,1792]{1,0:T(8,128)(2,1)S(1)} %get-tuple-element.27), channel_id=1, source_target_pairs={{0,3},{1,0},{2,1},{3,2},{4,7},{5,4},{6,5},{7,6},{8,11},{9,8},{10,9... | collective-permute-start | bytes 688136 | tf_op jit(solution)/shard_map/ppermute | solution.py:541
  137.8 5.9 %copy-start.11 = (bf16[64,1792]{1,0:T(8,128)(2,1)}, bf16[64,1792]{1,0:T(8,128)(2,1)S(1)}, u32[]{:S(2)}) copy-start(bf16[64,1792]{1,0:T(8,128)(2,1)S(1)} %collective-permute-done.7.refs_3_) | copy-start | bytes 688132
  144.5 9.6 %copy-start.19 = (bf16[64,1792]{1,0:T(8,128)(2,1)S(1)}, bf16[64,1792]{1,0:T(8,128)(2,1)}, u32[]{:S(2)}) copy-start(bf16[64,1792]{1,0:T(8,128)(2,1)} %get-tuple-element.21) | copy-start | bytes 688132
  144.5 31.8 %copy-start.22 = (bf16[64,128]{1,0:T(8,128)(2,1)S(1)}, bf16[64,128]{1,0:T(8,128)(2,1)}, u32[]{:S(2)}) copy-start(bf16[64,128]{1,0:T(8,128)(2,1)} %get-tuple-element.22) | copy-start | bytes 49156
  149.1 27.2 %all-to-all-start.5 = ((bf16[32,8,1792]{2,1,0:T(8,128)(2,1)}), bf16[32,8,1792]{2,1,0:T(8,128)(2,1)S(1)}, u32[]{:S(2)}, u32[]{:S(2)}) async-start(bf16[32,8,1792]{2,1,0:T(8,128)(2,1)} %bitcast.76), calls=%async_computation.5 | async-start | bytes 1835008 | tf_op jit(solution)/shard_map/all_to_all | solution.py:628
  (9 other events, 8.2 us)

commit v2 on v1

--- a/solution.py
+++ b/solution.py
@@ -37,7 +37,7 @@
 
 def quantize_kernel(top, held, scalars, factor, source, *rest):
     done = rest[:held]
-    out, weight, nat, rows, errs, levs, levels, lows, steps, scales, in_sem, out_sem, done_sem, bounce = rest[-14:]
+    out, weight, nat, rows, errs, levs, levels, lows, steps, scales, in_sem, out_sem, done_sem, back_sem, bounce = rest[-15:]
     columns = nat.shape[1]
     groups = columns // (SUBS * LANES)
     width = groups * SUBS
@@ -71,8 +71,20 @@
         steps[spot, :] = step
         scales[spot, :] = 1.0 / step
 
+    for copy in carried:
+        copy.wait()
+    returned = [pltpu.make_async_copy(bounce, out.at[pl.ds(0, top), :], back_sem) for _ in done]
+    for copy in returned:
+        copy.start()
+
+    def finish(b):
+        spot = b * BLK if isinstance(b, int) else pl.multiple_of(b * BLK, BLK)
+        return pltpu.make_async_copy(
+            levels.at[pl.ds(spot, BLK), :], out.at[pl.ds(top + spot, BLK), :], out_sem.at[b]
+        )
+
     def block_step(b, first_row):
-        base = pl.multiple_of(b * BLK, BLK)
+        base = b * BLK if isinstance(b, int) else pl.multiple_of(b * BLK, BLK)
         for g in range(width):
             rows[pl.ds(g, BLK, stride=width), :] = nat[
                 pl.ds(base, BLK), g * LANES : (g + 1) * LANES
@@ -108,28 +120,29 @@
 
             span = slice(c * SUBS * LANES, (c + 1) * SUBS * LANES)
             levels[pl.ds(base, BLK), span] = natural(levs).astype(levels.dtype)
+            if first_row == PANEL:
+                continue
             e1, e2, e3 = split_bf16(natural(errs))
             right = jnp.concatenate([e1, e2, e3, e1, e2, e1], axis=0)
             update = lax.dot_general(
                 left, right, (((0,), (0,)), ((), ())), preferred_element_type=jnp.float32
             )
             nat[first_row:, span] = nat[first_row:, span] - update
-
-    for begin in range(0, blocks, 2):
+        finish(b).start()
+
+    for begin in range(0, blocks - 2, 2):
 
         def body(b, carry):
             block_step(b, (begin + 1) * BLK)
             return carry
 
         lax.fori_loop(begin, begin + 2, body, 0)
-    store = pltpu.make_async_copy(levels, out.at[pl.ds(top, PANEL), :], out_sem)
-    store.start()
-    for copy in carried:
+    block_step(blocks - 2, (blocks - 1) * BLK)
+    block_step(blocks - 1, PANEL)
+    for b in range(blocks):
+        finish(b).wait()
+    for copy in returned:
         copy.wait()
-        back = pltpu.make_async_copy(bounce, out.at[pl.ds(0, top), :], done_sem)
-        back.start()
-        back.wait()
-    store.wait()
 
 
 def quantize_panel(index, factor, weight, partly, *after):
@@ -159,6 +172,7 @@
             small,
             small,
             pltpu.SemaphoreType.DMA((columns // (SUBS * LANES),)),
+            pltpu.SemaphoreType.DMA((PANEL // BLK,)),
             pltpu.SemaphoreType.DMA,
             pltpu.SemaphoreType.DMA,
             pltpu.VMEM((max(1, index) * PANEL, columns), jnp.bfloat16),
@@ -417,7 +431,7 @@
     )(packed, levels, *after)
 
 
-def route_kernel(owners, ids, gates, table, order, pick, combine):
+def route_kernel(owners, ids, gates, table, order, pick, combine, front, copies):
     picks, tokens = ids.shape
     first = pick.shape[1]
     experts = table.shape[1]
@@ -445,6 +459,9 @@
     place = jnp.where(picked > 0.0, ahead, count + token - ahead).astype(jnp.int32)
     moved = (row == place).astype(jnp.float32)
     order[...] = moved.astype(jnp.bfloat16)
+    front[...] = moved[:first].astype(jnp.bfloat16)
+    for chip in range(copies.shape[0] // first):
+        copies[chip * first : (chip + 1) * first, :] = moved[:first].astype(jnp.bfloat16)
     position = before(hit)
     spot = lax.broadcasted_iota(jnp.int32, (CAP, tokens), 0).astype(jnp.float32)
     chosen_rows, weighted = [], []
@@ -470,6 +487,8 @@
             jax.ShapeDtypeStruct((tokens, tokens), jnp.bfloat16),
             jax.ShapeDtypeStruct((slots, first), jnp.bfloat16),
             jax.ShapeDtypeStruct((slots, tokens), jnp.bfloat16),
+            jax.ShapeDtypeStruct((first, tokens), jnp.bfloat16),
+            jax.ShapeDtypeStruct((owners // 2 * first, tokens), jnp.bfloat16),
         ],
         cost_estimate=pl.CostEstimate(flops=10**7, bytes_accessed=10**5, transcendentals=0),
     )(expert_ids.T, gate_num.T, slot_table[None, :])
@@ -525,21 +544,27 @@
     return moved
 
 
-def to_other_ranks(chunks):
+def in_order_of_ranks(chunks):
     ranks = len(chunks)
     stacked = jnp.stack(chunks)
     chip = lax.div(lax.axis_index("dp"), 2)
     rank = lax.axis_index("tensor")
-    moved = []
+    ordered = []
     for shift in range(ranks):
         spot = jnp.bitwise_xor(chip, lax.rem(rank + shift, ranks))
         chunk = lax.dynamic_slice(
             stacked, (spot, 0, 0), (1,) + stacked.shape[1:], allow_negative_indices=False
-        )[0]
-        if shift:
-            pairs = [(place, (place + shift) % ranks) for place in range(ranks)]
-            chunk = lax.ppermute(chunk, "tensor", pairs)
-        moved.append(chunk)
+        )
+        ordered.append(chunk[0])
+    return ordered
+
+
+def to_other_ranks(chunks):
+    ranks = len(chunks)
+    moved = [chunks[0]]
+    for shift in range(1, ranks):
+        pairs = [(place, (place + shift) % ranks) for place in range(ranks)]
+        moved.append(lax.ppermute(chunks[shift], "tensor", pairs))
     return moved
 
 
@@ -572,13 +597,15 @@
     first = min(seq_len, owners * CAP) if chips == ranks == 4 else seq_len
     core = lax.rem(lax.axis_index("dp"), 2)[None]
     partner = lax.ppermute(out_proj, "dp", [(i, i ^ 1) for i in range(owners)])
-    order_rows, pick, combine = route(expert_ids, gate_num, slot_table, owners, first)
+    order_rows, pick, combine, order_first, order_copies = route(
+        expert_ids, gate_num, slot_table, owners, first
+    )
     factors = scaled_factors(inv_chol[0])
     weight = down_proj[0]
     panels = factors.shape[0]
     attended = attend(queries, latent, latent_up)
 
-    copies = chosen(jnp.tile(order_rows[:first], (chips, 1)), attended)
+    copies = chosen(order_copies, attended)
     everyone = across_chips(copies.reshape(chips, first, -1))
     later = []
     if first < seq_len and chips == ranks:
@@ -592,13 +619,11 @@
         later = project(core, later, out_proj, partner, partly[0])
     quantized = partly[0]
     front, outgoing = make_front(
-        across_ranks(arrived, ranks), order_rows[:first], residual_in, pick, quantized, *later
+        across_ranks(arrived, ranks), order_first, residual_in, pick, quantized
     )
     incoming = lax.all_to_all(
         outgoing.reshape(owners, CAP, -1), "dp", split_axis=0, concat_axis=0, tiled=True
     )
-    if later:
-        later = to_other_chips(later)
     packed = gate_and_up(
         incoming.reshape(owners * CAP, -1),
         norm_gain[None, :],
@@ -609,8 +634,10 @@
     )
     packed = lax.all_to_all(packed, "tensor", split_axis=0, concat_axis=0, tiled=True)
     if later:
+        later = in_order_of_ranks(to_other_chips(later))
+    expert_part, gram = expert_outputs(packed, quantized, model_cols * ranks, *later)
+    if later:
         later = to_other_ranks(later)
-    expert_part, gram = expert_outputs(packed, quantized, model_cols * ranks, *later)
     ordered_out = front
     if later:
         ordered_in = chosen(order_rows[first:], residual_in).astype(jnp.float32)

time: 179 us -> 172 us (0.961)
  waiting for transfers between devices: 58.6 us -> 52 us
  Pallas kernels: 58.2 us -> 56.3 us
    ppermute x3, waiting for transfers between devices: 21.6 us -> 0.01 us  [to_other_ranks(): moved.append(lax.ppermute(chunks[shift], 'tensor', pairs))]
    ppermute x6, waiting for transfers between devices: 1.16 us -> 7.85 us  [to_other_chips(): moved.append(lax.ppermute(chunks[turn], 'dp', pairs))]
    all_to_all x1, waiting for transfers between devices: 0.01 us -> 5.93 us  [shards(): lax.all_to_all(packed, 'tensor', split_axis=0, concat_axis=0, tiled=True)]
    convert_element_type x0 -> x1, other arithmetic: none -> 1.97 us  [shards(): ordered_out = jnp.concatenate([front, back.astype(jnp.bfloat16)], axis=0)]
    unnamed x48 -> x38, local copies, waits for them, and re-layouts: 4.88 us -> 4.82 us
  transfers between devices with their start and end apart: 16 -> 16, of which waited for: 7 -> 6; matrix products, arithmetic and copies ran while one was open for 9% -> 10% of each run, Pallas kernels for 23% -> 26%
where the time goes in v2:
time: 172 us; the launch traced here: 170 us
  Pallas kernels  56.3 us (33%)
  waiting for transfers between devices  52 us (30%)
  starting transfers between devices  37.9 us (22%)
  matrix products  12.6 us (7%)
  local copies, waits for them, and re-layouts  7.15 us (4%)
  other arithmetic  3.3 us (2%)
    pallas_call x2, Pallas kernels, quantize_panel(): pl.pallas_call(lambda *refs: quantize_kernel(index * PANEL, len(partly),...  28.6 us
    all_to_all x1, waiting for transfers between devices, shards(): lax.all_to_all(parcels, ('dp', 'tensor'), split_axis=0, concat_axis=0, ti...  22.5 us
    pallas_call x2, Pallas kernels, project(): pl.pallas_call(lambda *refs: project_kernel(len(rows), *refs), out_shape=...  14 us
    all_to_all x2, waiting for transfers between devices, across_chips(): lax.all_to_all(chunks, 'dp', split_axis=0, concat_axis=0, axis_index_grou...  10 us
    all_to_all x2, starting transfers between devices, across_chips(): lax.all_to_all(chunks, 'dp', split_axis=0, concat_axis=0, axis_index_grou...  8.12 us
    ppermute x6, waiting for transfers between devices, to_other_chips(): moved.append(lax.ppermute(chunks[turn], 'dp', pairs))  7.85 us
    ppermute x6, starting transfers between devices, to_other_chips(): moved.append(lax.ppermute(chunks[turn], 'dp', pairs))  7.18 us
    all_to_all x1, waiting for transfers between devices, shards(): lax.all_to_all(packed, 'tensor', split_axis=0, concat_axis=0, tiled=True)  5.93 us
  transfers between devices with their start and end apart: 16, of which 6 were waited for; matrix products, arithmetic and copies ran while one was open for 10% of the time, Pallas kernels for 26%

profile of v2, /device:TPU:8, one launch (start us, length us, event | category | flops | bytes accessed | tf_op | source)
XLA Modules:
  0.0 170.2 jit_solution(11710559969733432420)
XLA Ops:
  0.7 3.1 %convolution_convert_fusion.5 = bf16[128,16,256]{2,0,1:T(8,128)(2,1)S(1)} fusion(bf16[16,512,256]{2,1,0:T(8,128)(2,1)} %param.16, bf16[128,576]{0,1:T(8,128)(2,1)} %param.15), kind=kOutput, calls=%fused_computation.7 | convolution fusion | flops 537395200 | bytes 5373952 | tf_op jit(solution)/shard_map/tc,hcd->thd/dot_general | solution.py:506
  4.0 1.7 shard_map.156
  6.4 1.4 fusion.5
  7.8 2.1 %convolution_convert_fusion.6 = bf16[16,128,128]{2,1,0:T(8,128)(2,1)S(1)} fusion(bf16[128,16,256]{2,0,1:T(8,128)(2,1)S(1)} %convolution_convert_fusion.5, f32[16,128]{1,0:T(8,128)S(1)} %fusion.28, f32[16,128,128]{1,2,0:T(8,128)} %fusion.5), kind=kOutput, calls=%fused_computation.13 | convolution fusion | flops 68159616 | bytes 3153920 | tf_op jit(solution)/shard_map/hts,shd->thd/dot_general | solution.py:517
  9.9 1.4 convolution_convert_fusion.refs_3_
  11.3 3.7 %all-to-all-start = ((bf16[4,64,2048]{2,1,0:T(8,128)(2,1)}), bf16[4,64,2048]{2,1,0:T(8,128)(2,1)S(1)}, u32[]{:S(2)}, u32[]{:S(2)}) async-start(bf16[4,64,2048]{2,1,0:T(8,128)(2,1)} %bitcast.8), calls=%async_computation | async-start | bytes 2097152 | tf_op jit(solution)/shard_map/all_to_all | solution.py:533
  17.0 14.0 %shard_map.157.refs_4_.refs_3_ = bf16[128,7168]{1,0:T(8,128)(2,1)} custom-call(f32[128,128]{1,0:T(8,128)} %get-tuple-element.35.refs_0_.refs_1_, f32[128,128]{1,0:T(8,128)} %get-tuple-element.35.refs_0_.refs_1_, bf16[256,7168]{1,0:T(8,128)(2,1)} %bitcast.87, bf16[256,2048]{1,0:T(8,128)(2,1)} %convolution_convert_fusion.refs_3_, ...), custom_call_target="tpu_custom_call" | custom-call | flops 16000000000 | bytes 3670016 | tf_op jit(solution)/shard_map/pallas_call | solution.py:154
  32.1 7.0 %shard_map.158.refs_4_ = bf16[4,64,1792]{2,1,0:T(8,128)(2,1)} custom-call(s32[1]{0:T(128)} %bitcast.3.refs_0_, bf16[2048,896]{1,0:T(8,128)(2,1)} %refs_1_.3, bf16[2048,896]{1,0:T(8,128)(2,1)} %collective-permute-done.refs_2_, bf16[4,64,2048]{2,1,0:T(8,128)(2,1)} %copy-done.1, bf16[128,7168]{1,0:T(8,128)(2,1)} %shard_map.157.refs_4_.refs_3_), custom_call_target="tpu_custom_call" | custom-call | flops 1879048192 | bytes 9306112 | tf_op jit(solution)/shard_map/pallas_call | solution.py:249
  39.1 4.4 %all-to-all-start.1 = ((bf16[4,64,1792]{2,1,0:T(8,128)(2,1)}), bf16[4,64,1792]{2,1,0:T(8,128)(2,1)}, u32[]{:S(2)}, u32[]{:S(2)}) async-start(bf16[4,64,1792]{2,1,0:T(8,128)(2,1)} %shard_map.158.refs_4_), calls=%async_computation.1 | async-start | bytes 1835008 | tf_op jit(solution)/shard_map/all_to_all | solution.py:533
  43.5 2.1 %collective-permute-start.1 = (bf16[64,2048]{1,0:T(8,128)(2,1)S(1)}, bf16[64,2048]{1,0:T(8,128)(2,1)S(1)}, u32[]{:S(2)}, u32[]{:S(2)}) collective-permute-start(bf16[64,2048]{1,0:T(8,128)(2,1)S(1)} %copy-done.5), channel_id=1, source_target_pairs={{0,8},{4,12},{8,0},{12,4},{16,24},{20,28},{24,16},{28,20},{1,9},{5... | collective-permute-start | bytes 786440 | tf_op jit(solution)/shard_map/ppermute | solution.py:543
  45.6 1.4 collective-permute-start.2
  47.2 10.0 %all-to-all-done.1 = bf16[4,64,1792]{2,1,0:T(8,128)(2,1)} async-done(((bf16[4,64,1792]{2,1,0:T(8,128)(2,1)}), bf16[4,64,1792]{2,1,0:T(8,128)(2,1)}, u32[]{:S(2)}, u32[]{:S(2)}) %all-to-all-start.1) | async-done | bytes 917536 | tf_op jit(solution)/shard_map/all_to_all | solution.py:533
  57.2 5.3 %all-to-all-start.2 = ((bf16[4,1,64,1792]{3,2,1,0:T(8,128)(2,1)}), bf16[4,1,64,1792]{3,2,1,0:T(8,128)(2,1)S(1)}, u32[]{:S(2)}, u32[]{:S(2)}) async-start(bf16[4,1,64,1792]{3,2,1,0:T(8,128)(2,1)} %bitcast.15), calls=%async_computation.2 | async-start | bytes 1835008 | tf_op jit(solution)/shard_map/all_to_all | solution.py:574
  62.5 14.5 %shard_map.159.rest_0_.refs_7_.refs_1_ = bf16[256,7168]{1,0:T(8,128)(2,1)} custom-call(f32[128,128]{1,0:T(8,128)} %get-tuple-element.36.refs_0_.refs_1_, f32[128,128]{1,0:T(8,128)} %get-tuple-element.36.refs_0_.refs_1_, bf16[256,7168]{1,0:T(8,128)(2,1)} %bitcast.88, bf16[128,7168]{1,0:T(8,128)(2,1)} %shard_map.157.refs_4_.refs_3_, ...), custom_call_target="tpu_custom_call" | custom-call | flops 16000000000 | bytes 3670016 | tf_op jit(solution)/shard_map/pallas_call | solution.py:154
  78.6 6.9 %shard_map.161 = (bf16[64,1792]{1,0:T(8,128)(2,1)}, bf16[64,1792]{1,0:T(8,128)(2,1)}, bf16[64,1792]{1,0:T(8,128)(2,1)}, bf16[64,1792]{1,0:T(8,128)(2,1)}) custom-call(s32[1]{0:T(128)} %bitcast.3.refs_0_, bf16[2048,896]{1,0:T(8,128)(2,1)} %refs_1_.3, bf16[2048,896]{1,0:T(8,128)(2,1)} %collective-permute-done.refs_2_, ...), custom_call_target="tpu_custom_call" | custom-call | flops 1879048192 | bytes 9306112 | tf_op jit(solution)/shard_map/pallas_call | solution.py:249
  85.6 1.5 collective-permute-start.4
  87.6 1.5 collective-permute-start.6
  89.7 4.2 %collective-permute-done.4 = bf16[64,1792]{1,0:T(8,128)(2,1)S(1)} collective-permute-done((bf16[64,1792]{1,0:T(8,128)(2,1)}, bf16[64,1792]{1,0:T(8,128)(2,1)S(1)}, u32[]{:S(2)}, u32[]{:S(2)}) %collective-permute-start.4) | collective-permute-done | bytes 229408 | tf_op jit(solution)/shard_map/ppermute | solution.py:543
  94.0 3.6 %collective-permute-done.5 = bf16[64,1792]{1,0:T(8,128)(2,1)S(1)} collective-permute-done((bf16[64,1792]{1,0:T(8,128)(2,1)}, bf16[64,1792]{1,0:T(8,128)(2,1)S(1)}, u32[]{:S(2)}, u32[]{:S(2)}) %collective-permute-start.5) | collective-permute-done | bytes 229408 | tf_op jit(solution)/shard_map/ppermute | solution.py:543
  99.4 1.5 collective-permute-start.7
  100.9 1.2 collective-permute-start.8
  102.0 1.8 %collective-permute-start.9 = (bf16[64,1792]{1,0:T(8,128)(2,1)S(1)}, bf16[64,1792]{1,0:T(8,128)(2,1)}, u32[]{:S(2)}, u32[]{:S(2)}) collective-permute-start(bf16[64,1792]{1,0:T(8,128)(2,1)S(1)} %get-tuple-element.33.refs_5_), channel_id=1, source_target_pairs={{0,3},{1,0},{2,1},{3,2},{4,7},{5,4},{6,5},{7,6},{8,11},{9,8},{10,9... | collective-permute-start | bytes 688136 | tf_op jit(solution)/shard_map/ppermute | solution.py:567
  104.7 2.4 %shard_map.160 = (bf16[64,1792]{1,0:T(8,128)(2,1)}, bf16[64,1792]{1,0:T(8,128)(2,1)}) custom-call(bf16[4,1,64,1792]{3,2,1,0:T(8,128)(2,1)} %copy-done.2, bf16[64,128]{1,0:T(8,128)(2,1)} %get-tuple-element.19.order, bf16[128,1792]{1,0:T(8,128)(2,1)} %residual.1, bf16[64,64]{1,0:T(8,128)(2,1)} %get-tuple-element.20.pick, ...), custom_call_target="tpu_custom_call" | custom-call | flops 100000000 | bytes 917504 | tf_op jit(solution)/shard_map/pallas_call | solution.py:288
  107.1 3.4 %all-to-all-start.3 = ((bf16[8,8,1792]{2,1,0:T(8,128)(2,1)}), bf16[8,8,1792]{2,1,0:T(8,128)(2,1)S(1)}, u32[]{:S(2)}, u32[]{:S(2)}) async-start(bf16[8,8,1792]{2,1,0:T(8,128)(2,1)} %bitcast.83), calls=%async_computation.3 | async-start | bytes 458752 | tf_op jit(solution)/shard_map/all_to_all | solution.py:624
  111.4 5.6 %all-to-all-done.3 = bf16[8,8,1792]{2,1,0:T(8,128)(2,1)S(1)} async-done(((bf16[8,8,1792]{2,1,0:T(8,128)(2,1)}), bf16[8,8,1792]{2,1,0:T(8,128)(2,1)S(1)}, u32[]{:S(2)}, u32[]{:S(2)}) %all-to-all-start.3) | async-done | bytes 229408 | tf_op jit(solution)/shard_map/all_to_all | solution.py:624
  117.7 5.1 %shard_map.162 = bf16[4,64,640]{2,1,0:T(8,128)(2,1)} custom-call(bf16[64,1792]{1,0:T(8,128)(2,1)} %bitcast.77, bf16[1,1792]{1,0:T(2,128)(2,1)} %broadcast_in_dim.78.gain, bf16[1792,1024]{1,0:T(8,128)(2,1)} %bitcast.71, bf16[1792,1024]{1,0:T(8,128)(2,1)} %bitcast.72, bf16[64,1792]{1,0:T(8,128)(2,1)} %get-tuple-element.22.rest_0_, ...), custom_call_target="tpu_custom_call" | custom-call | flops 469762048 | bytes 7340032 | tf_op jit(solution)/shard_map/pallas_call | solution.py:348
  122.8 4.9 %all-to-all-start.4 = ((bf16[4,64,640]{2,1,0:T(8,128)(2,1)}), bf16[4,64,640]{2,1,0:T(8,128)(2,1)S(1)}, u32[]{:S(2)}, u32[]{:S(2)}) async-start(bf16[4,64,640]{2,1,0:T(8,128)(2,1)} %shard_map.162), calls=%async_computation.4 | async-start | bytes 655360 | tf_op jit(solution)/shard_map/all_to_all | solution.py:635
  127.7 2.0 %add_convert_fusion = (bf16[64,1792]{1,0:T(8,128)(2,1)S(1)}, bf16[64,1792]{1,0:T(8,128)(2,1)}) fusion(f32[64,1792]{1,0:T(8,128)S(1)} %fusion.1, bf16[64,1792]{1,0:T(8,128)(2,1)} %collective-permute-done.9, bf16[64,1792]{1,0:T(8,128)(2,1)} %collective-permute-done.8, bf16[64,1792]{1,0:T(8,128)(2,1)} %collective-permute-done.7, ...), kind=kLoop, calls=%fused_computation.25 | loop fusion | flops 1032192 | bytes 1835012 | tf_op jit(solution)/shard_map/convert_element_type | solution.py:645
  129.7 5.9 %all-to-all-done.4.refs_0_ = bf16[4,64,640]{2,1,0:T(8,128)(2,1)S(1)} async-done(((bf16[4,64,640]{2,1,0:T(8,128)(2,1)}), bf16[4,64,640]{2,1,0:T(8,128)(2,1)S(1)}, u32[]{:S(2)}, u32[]{:S(2)}) %all-to-all-start.4) | async-done | bytes 327712 | tf_op jit(solution)/shard_map/all_to_all | solution.py:635
  136.4 4.5 %shard_map.163 = (bf16[64,7168]{1,0:T(8,128)(2,1)}, f32[256,128]{1,0:T(8,128)}) custom-call(bf16[4,64,640]{2,1,0:T(8,128)(2,1)} %copy-done.4, bf16[256,7168]{1,0:T(8,128)(2,1)} %shard_map.159.rest_0_.refs_7_.refs_1_, bf16[64,1792]{1,0:T(8,128)(2,1)} %get-tuple-element.31.refs_2_, bf16[64,1792]{1,0:T(8,128)(2,1)} %copy-done.7, ...), custom_call_target="tpu_custom_call" | custom-call | flops 234881024 | bytes 3670016 | tf_op jit(solution)/shard_map/pallas_call | solution.py:413
  140.9 4.5 %all-to-all-start.5 = ((bf16[32,8,1792]{2,1,0:T(8,128)(2,1)}), bf16[32,8,1792]{2,1,0:T(8,128)(2,1)S(1)}, u32[]{:S(2)}, u32[]{:S(2)}) async-start(bf16[32,8,1792]{2,1,0:T(8,128)(2,1)} %bitcast.75), calls=%async_computation.5 | async-start | bytes 1835008 | tf_op jit(solution)/shard_map/all_to_all | solution.py:655
  146.5 22.5 %all-to-all-done.5 = bf16[32,8,1792]{2,1,0:T(8,128)(2,1)S(1)} async-done(((bf16[32,8,1792]{2,1,0:T(8,128)(2,1)}), bf16[32,8,1792]{2,1,0:T(8,128)(2,1)S(1)}, u32[]{:S(2)}, u32[]{:S(2)}) %all-to-all-start.5) | async-done | bytes 917536 | tf_op jit(solution)/shard_map/all_to_all | solution.py:655
  (72 shorter events, 13.9 us)
Async XLA Ops:
  0.6 5.2 %copy-start = (bf16[128,16,192]{0,2,1:T(8,128)(2,1)S(1)}, bf16[128,16,192]{0,2,1:T(8,128)(2,1)}, u32[]{:S(2)}) copy-start(bf16[128,16,192]{0,2,1:T(8,128)(2,1)} %param.14) | copy-start | bytes 2359300
  0.6 3.3 %slice-start = ((bf16[128,576]{0,1:T(8,128)(2,1)}), bf16[128,64]{0,1:T(8,128)(2,1)S(1)}, s32[]{:S(2)}) async-start(bf16[128,576]{0,1:T(8,128)(2,1)} %param.15), calls=%async_computation.6 | async-start | bytes 32768 | tf_op jit(solution)/shard_map/slice | solution.py:509
  0.7 30.4 %collective-permute-start = (bf16[2048,896]{1,0:T(8,128)(2,1)}, bf16[2048,896]{1,0:T(8,128)(2,1)}, u32[]{:S(2)}, u32[]{:S(2)}) collective-permute-start(bf16[2048,896]{1,0:T(8,128)(2,1)} %refs_1_.3), channel_id=1, source_target_pairs={{0,4},{4,0},{8,12},{12,8},{16,20},{20,16},{24,28},{28,24},{1,5},{5... | collective-permute-start | bytes 11010056 | tf_op jit(solution)/shard_map/ppermute | solution.py:599
  6.4 3.5 %copy-start.16 = (bf16[256,128]{1,0:T(8,128)(2,1)S(1)}, bf16[256,128]{1,0:T(8,128)(2,1)}, u32[]{:S(2)}) copy-start(bf16[256,128]{1,0:T(8,128)(2,1)} %get-tuple-element.18) | copy-start | bytes 196612
  7.8 7.3 %copy-start.9 = (f32[1,256,128]{2,1,0:T(8,128)S(1)}, f32[1,256,128]{2,1,0:T(8,128)}, u32[]{:S(2)}) copy-start(f32[1,256,128]{2,1,0:T(8,128)} %param.25) | copy-start | bytes 393220
  7.8 8.2 %copy-start.14 = (bf16[128,128]{1,0:T(8,128)(2,1)S(1)}, bf16[128,128]{1,0:T(8,128)(2,1)}, u32[]{:S(2)}) copy-start(bf16[128,128]{1,0:T(8,128)(2,1)} %get-tuple-element.17) | copy-start | bytes 98308
  11.3 19.8 %all-to-all-start = ((bf16[4,64,2048]{2,1,0:T(8,128)(2,1)}), bf16[4,64,2048]{2,1,0:T(8,128)(2,1)S(1)}, u32[]{:S(2)}, u32[]{:S(2)}) async-start(bf16[4,64,2048]{2,1,0:T(8,128)(2,1)} %bitcast.8), calls=%async_computation | async-start | bytes 2097152 | tf_op jit(solution)/shard_map/all_to_all | solution.py:533
  31.1 1.0 copy-start.1
  32.1 11.5 %copy-start.5 = (bf16[64,2048]{1,0:T(8,128)(2,1)S(1)}, bf16[64,2048]{1,0:T(8,128)(2,1)}, u32[]{:S(2)}) copy-start(bf16[64,2048]{1,0:T(8,128)(2,1)} %convolution_convert_fusion.4.refs_4_.refs_3_) | copy-start | bytes 786436
  39.1 18.1 %all-to-all-start.1 = ((bf16[4,64,1792]{2,1,0:T(8,128)(2,1)}), bf16[4,64,1792]{2,1,0:T(8,128)(2,1)}, u32[]{:S(2)}, u32[]{:S(2)}) async-start(bf16[4,64,1792]{2,1,0:T(8,128)(2,1)} %shard_map.158.refs_4_), calls=%async_computation.1 | async-start | bytes 1835008 | tf_op jit(solution)/shard_map/all_to_all | solution.py:533
  43.5 33.6 %collective-permute-start.1 = (bf16[64,2048]{1,0:T(8,128)(2,1)S(1)}, bf16[64,2048]{1,0:T(8,128)(2,1)S(1)}, u32[]{:S(2)}, u32[]{:S(2)}) collective-permute-start(bf16[64,2048]{1,0:T(8,128)(2,1)S(1)} %copy-done.5), channel_id=1, source_target_pairs={{0,8},{4,12},{8,0},{12,4},{16,24},{20,28},{24,16},{28,20},{1,9},{5... | collective-permute-start | bytes 786440 | tf_op jit(solution)/shard_map/ppermute | solution.py:543
  45.6 31.5 %collective-permute-start.2 = (bf16[64,2048]{1,0:T(8,128)(2,1)S(1)}, bf16[64,2048]{1,0:T(8,128)(2,1)S(1)}, u32[]{:S(2)}, u32[]{:S(2)}) collective-permute-start(bf16[64,2048]{1,0:T(8,128)(2,1)S(1)} %copy-done.5), channel_id=1, source_target_pairs={{0,16},{4,20},{8,24},{12,28},{16,0},{20,4},{24,8},{28,12},{1,17},{... | collective-permute-start | bytes 786440 | tf_op jit(solution)/shard_map/ppermute | solution.py:543
  47.1 30.1 %collective-permute-start.3 = (bf16[64,2048]{1,0:T(8,128)(2,1)S(1)}, bf16[64,2048]{1,0:T(8,128)(2,1)S(1)}, u32[]{:S(2)}, u32[]{:S(2)}) collective-permute-start(bf16[64,2048]{1,0:T(8,128)(2,1)S(1)} %copy-done.5), channel_id=1, source_target_pairs={{0,24},{4,28},{8,16},{12,20},{16,8},{20,12},{24,0},{28,4},{1,25},{... | collective-permute-start | bytes 786440 | tf_op jit(solution)/shard_map/ppermute | solution.py:543
  57.2 46.6 %all-to-all-start.2 = ((bf16[4,1,64,1792]{3,2,1,0:T(8,128)(2,1)}), bf16[4,1,64,1792]{3,2,1,0:T(8,128)(2,1)S(1)}, u32[]{:S(2)}, u32[]{:S(2)}) async-start(bf16[4,1,64,1792]{3,2,1,0:T(8,128)(2,1)} %bitcast.15), calls=%async_computation.2 | async-start | bytes 1835008 | tf_op jit(solution)/shard_map/all_to_all | solution.py:574
  77.1 12.0 %copy-start.18 = (bf16[1792]{0:T(1024)(128)(2,1)S(1)}, bf16[1792]{0:T(1024)(128)(2,1)}, u32[]{:S(2)}) copy-start(bf16[1792]{0:T(1024)(128)(2,1)} %param.18) | copy-start | bytes 10756
  77.1 0.8 copy-start.11
  85.6 8.4 %collective-permute-start.4 = (bf16[64,1792]{1,0:T(8,128)(2,1)}, bf16[64,1792]{1,0:T(8,128)(2,1)S(1)}, u32[]{:S(2)}, u32[]{:S(2)}) collective-permute-start(bf16[64,1792]{1,0:T(8,128)(2,1)} %get-tuple-element.23.rest_1_), channel_id=1, source_target_pairs={{0,8},{4,12},{8,0},{12,4},{16,24},{20,28},{24,16},{28,20},{1,9},{5... | collective-permute-start | bytes 688136 | tf_op jit(solution)/shard_map/ppermute | solution.py:543
  87.1 10.5 %collective-permute-start.5 = (bf16[64,1792]{1,0:T(8,128)(2,1)}, bf16[64,1792]{1,0:T(8,128)(2,1)S(1)}, u32[]{:S(2)}, u32[]{:S(2)}) collective-permute-start(bf16[64,1792]{1,0:T(8,128)(2,1)} %get-tuple-element.24.rest_2_), channel_id=1, source_target_pairs={{0,16},{4,20},{8,24},{12,28},{16,0},{20,4},{24,8},{28,12},{1,17},{... | collective-permute-start | bytes 688136 | tf_op jit(solution)/shard_map/ppermute | solution.py:543
  87.6 9.9 %collective-permute-start.6 = (bf16[64,1792]{1,0:T(8,128)(2,1)}, bf16[64,1792]{1,0:T(8,128)(2,1)S(1)}, u32[]{:S(2)}, u32[]{:S(2)}) collective-permute-start(bf16[64,1792]{1,0:T(8,128)(2,1)} %get-tuple-element.25.rest_3_), channel_id=1, source_target_pairs={{0,24},{4,28},{8,16},{12,20},{16,8},{20,12},{24,0},{28,4},{1,25},{... | collective-permute-start | bytes 688136 | tf_op jit(solution)/shard_map/ppermute | solution.py:543
  98.6 11.9 %copy-start.3 = (bf16[128,1792]{1,0:T(8,128)(2,1)S(1)}, bf16[128,1792]{1,0:T(8,128)(2,1)}, u32[]{:S(2)}) copy-start(bf16[128,1792]{1,0:T(8,128)(2,1)} %residual.1) | copy-start | bytes 1376260
  99.4 36.3 %copy-start.7 = (bf16[64,1792]{1,0:T(8,128)(2,1)}, bf16[64,1792]{1,0:T(8,128)(2,1)S(1)}, u32[]{:S(2)}) copy-start(bf16[64,1792]{1,0:T(8,128)(2,1)S(1)} %get-tuple-element.32.refs_3_) | copy-start | bytes 688132
  99.4 36.3 %copy-start.8 = (bf16[64,1792]{1,0:T(8,128)(2,1)}, bf16[64,1792]{1,0:T(8,128)(2,1)S(1)}, u32[]{:S(2)}) copy-start(bf16[64,1792]{1,0:T(8,128)(2,1)S(1)} %get-tuple-element.33.refs_5_) | copy-start | bytes 688132
  99.4 28.3 %collective-permute-start.7 = (bf16[64,1792]{1,0:T(8,128)(2,1)S(1)}, bf16[64,1792]{1,0:T(8,128)(2,1)}, u32[]{:S(2)}, u32[]{:S(2)}) collective-permute-start(bf16[64,1792]{1,0:T(8,128)(2,1)S(1)} %get-tuple-element.32.refs_3_), channel_id=1, source_target_pairs={{0,1},{1,2},{2,3},{3,0},{4,5},{5,6},{6,7},{7,4},{8,9},{9,10},{10,1... | collective-permute-start | bytes 688136 | tf_op jit(solution)/shard_map/ppermute | solution.py:567
  100.9 26.9 %collective-permute-start.8 = (bf16[64,1792]{1,0:T(8,128)(2,1)}, bf16[64,1792]{1,0:T(8,128)(2,1)}, u32[]{:S(2)}, u32[]{:S(2)}) collective-permute-start(bf16[64,1792]{1,0:T(8,128)(2,1)} %get-tuple-element.34.refs_4_), channel_id=1, source_target_pairs={{0,2},{1,3},{2,0},{3,1},{4,6},{5,7},{6,4},{7,5},{8,10},{9,11},{10,... | collective-permute-start | bytes 688136 | tf_op jit(solution)/shard_map/ppermute | solution.py:567
  102.0 25.7 %collective-permute-start.9 = (bf16[64,1792]{1,0:T(8,128)(2,1)S(1)}, bf16[64,1792]{1,0:T(8,128)(2,1)}, u32[]{:S(2)}, u32[]{:S(2)}) collective-permute-start(bf16[64,1792]{1,0:T(8,128)(2,1)S(1)} %get-tuple-element.33.refs_5_), channel_id=1, source_target_pairs={{0,3},{1,0},{2,1},{3,2},{4,7},{5,4},{6,5},{7,6},{8,11},{9,8},{10,9... | collective-permute-start | bytes 688136 | tf_op jit(solution)/shard_map/ppermute | solution.py:567
  103.8 0.9 copy-start.2
  107.1 9.9 %all-to-all-start.3 = ((bf16[8,8,1792]{2,1,0:T(8,128)(2,1)}), bf16[8,8,1792]{2,1,0:T(8,128)(2,1)S(1)}, u32[]{:S(2)}, u32[]{:S(2)}) async-start(bf16[8,8,1792]{2,1,0:T(8,128)(2,1)} %bitcast.83), calls=%async_computation.3 | async-start | bytes 458752 | tf_op jit(solution)/shard_map/all_to_all | solution.py:624
  122.8 12.8 %all-to-all-start.4 = ((bf16[4,64,640]{2,1,0:T(8,128)(2,1)}), bf16[4,64,640]{2,1,0:T(8,128)(2,1)S(1)}, u32[]{:S(2)}, u32[]{:S(2)}) async-start(bf16[4,64,640]{2,1,0:T(8,128)(2,1)} %shard_map.162), calls=%async_computation.4 | async-start | bytes 655360 | tf_op jit(solution)/shard_map/all_to_all | solution.py:635
  129.7 15.7 %copy-start.13 = (bf16[64,1792]{1,0:T(8,128)(2,1)S(1)}, bf16[64,1792]{1,0:T(8,128)(2,1)}, u32[]{:S(2)}) copy-start(bf16[64,1792]{1,0:T(8,128)(2,1)} %get-tuple-element.21) | copy-start | bytes 688132
  129.7 15.7 %copy-start.15 = (bf16[128,128]{1,0:T(8,128)(2,1)S(1)}, bf16[128,128]{1,0:T(8,128)(2,1)}, u32[]{:S(2)}) copy-start(bf16[128,128]{1,0:T(8,128)(2,1)} %get-tuple-element.17) | copy-start | bytes 98308
  136.4 32.7 %copy-start.17 = (bf16[64,128]{1,0:T(8,128)(2,1)S(1)}, bf16[64,128]{1,0:T(8,128)(2,1)}, u32[]{:S(2)}) copy-start(bf16[64,128]{1,0:T(8,128)(2,1)} %get-tuple-element.26) | copy-start | bytes 49156
  140.9 28.2 %all-to-all-start.5 = ((bf16[32,8,1792]{2,1,0:T(8,128)(2,1)}), bf16[32,8,1792]{2,1,0:T(8,128)(2,1)S(1)}, u32[]{:S(2)}, u32[]{:S(2)}) async-start(bf16[32,8,1792]{2,1,0:T(8,128)(2,1)} %bitcast.75), calls=%async_computation.5 | async-start | bytes 1835008 | tf_op jit(solution)/shard_map/all_to_all | solution.py:655
  (4 other events, 2.8 us)

commit v3 on v2

--- a/solution.py
+++ b/solution.py
@@ -300,6 +300,32 @@
     )(arrived, order, residual, pick, *after)
 
 
+def arrange_kernel(count, spots, *rest):
+    chunks, outs = rest[:count], rest[-count:]
+    for place, out in enumerate(outs):
+        for number, chunk in enumerate(chunks):
+
+            @pl.when(spots[place] == number)
+            def _():
+                out[...] = chunk[...]
+
+
+def arrange(spots, chunks, *after):
+    vmem = pl.BlockSpec(memory_space=pltpu.VMEM)
+    return pl.pallas_call(
+        lambda *refs: arrange_kernel(len(chunks), *refs),
+        out_shape=[jax.ShapeDtypeStruct(chunk.shape, chunk.dtype) for chunk in chunks],
+        in_specs=[pl.BlockSpec(memory_space=pltpu.SMEM)]
+        + [vmem] * len(chunks)
+        + [pl.BlockSpec(memory_space=pl.ANY)] * len(after),
+        out_specs=[vmem] * len(chunks),
+        compiler_params=pltpu.CompilerParams(vmem_limit_bytes=VMEM_LIMIT),
+        cost_estimate=pl.CostEstimate(
+            flops=0, bytes_accessed=4 * len(chunks) * chunks[0].size, transcendentals=0
+        ),
+    )(spots, *chunks, *after)
+
+
 def gate_kernel(rows, gain, gate_w, up_w, *rest):
     packed, weights, gate, up, scaled, sem = rest[-6:]
     tiles = sem.shape[1]
@@ -544,19 +570,11 @@
     return moved
 
 
-def in_order_of_ranks(chunks):
+def in_order_of_ranks(chunks, after):
     ranks = len(chunks)
-    stacked = jnp.stack(chunks)
     chip = lax.div(lax.axis_index("dp"), 2)
-    rank = lax.axis_index("tensor")
-    ordered = []
-    for shift in range(ranks):
-        spot = jnp.bitwise_xor(chip, lax.rem(rank + shift, ranks))
-        chunk = lax.dynamic_slice(
-            stacked, (spot, 0, 0), (1,) + stacked.shape[1:], allow_negative_indices=False
-        )
-        ordered.append(chunk[0])
-    return ordered
+    turned = lax.rem(lax.axis_index("tensor") + jnp.arange(ranks, dtype=jnp.int32), ranks)
+    return arrange(jnp.bitwise_xor(chip, turned), chunks, after)
 
 
 def to_other_ranks(chunks):
@@ -634,7 +652,7 @@
     )
     packed = lax.all_to_all(packed, "tensor", split_axis=0, concat_axis=0, tiled=True)
     if later:
-        later = in_order_of_ranks(to_other_chips(later))
+        later = in_order_of_ranks(to_other_chips(later), outgoing)
     expert_part, gram = expert_outputs(packed, quantized, model_cols * ranks, *later)
     if later:
         later = to_other_ranks(later)

time: 172 us -> 183 us (1.064)
  waiting for transfers between devices: 52 us -> 61.1 us
  Pallas kernels: 56.3 us -> 58.8 us
  other arithmetic: 3.3 us -> 0.92 us
  starting transfers between devices: 37.9 us -> 40.1 us
    ppermute x3, waiting for transfers between devices: 0.01 us -> 37.2 us  [to_other_ranks(): moved.append(lax.ppermute(chunks[shift], 'tensor', pairs))]
    all_to_all x1, waiting for transfers between devices: 22.5 us -> 0.01 us  [shards(): lax.all_to_all(parcels, ('dp', 'tensor'), split_axis=0, concat_axis=0, ti...]
    all_to_all x1, waiting for transfers between devices: 5.93 us -> 0.01 us  [shards(): lax.all_to_all(packed, 'tensor', split_axis=0, concat_axis=0, tiled=True)]
    all_to_all x1, waiting for transfers between devices: 5.58 us -> 0.01 us  [shards(): lax.all_to_all(outgoing.reshape(owners, CAP, -1), 'dp', split_axis=0, con...]
    all_to_all x1, waiting for transfers between devices: 0.01 us -> 3.95 us  [across_ranks(): lax.all_to_all(chunks, 'tensor', split_axis=0, concat_axis=0, tiled=True)]
    pallas_call x0 -> x1, Pallas kernels: none -> 2.39 us  [arrange(): pl.pallas_call(lambda *refs: arrange_kernel(len(chunks), *refs), out_shap...]
    ppermute x6, waiting for transfers between devices: 7.85 us -> 9.89 us  [to_other_chips(): moved.append(lax.ppermute(chunks[turn], 'dp', pairs))]
    all_to_all x1, starting transfers between devices: 4.89 us -> 6.74 us  [shards(): lax.all_to_all(packed, 'tensor', split_axis=0, concat_axis=0, tiled=True)]
  transfers between devices with their start and end apart: 16 -> 16, of which waited for: 6 -> 7; matrix products, arithmetic and copies ran while one was open for 10% -> 7% of each run, Pallas kernels for 26% -> 23%
where the time goes in v3:
time: 183 us; the launch traced here: 182 us
  waiting for transfers between devices  61.1 us (33%)
  Pallas kernels  58.8 us (32%)
  starting transfers between devices  40.1 us (22%)
  matrix products  11.9 us (7%)
  local copies, waits for them, and re-layouts  7.77 us (4%)
    ppermute x3, waiting for transfers between devices, to_other_ranks(): moved.append(lax.ppermute(chunks[shift], 'tensor', pairs))  37.2 us
    pallas_call x2, Pallas kernels, quantize_panel(): pl.pallas_call(lambda *refs: quantize_kernel(index * PANEL, len(partly),...  28.6 us
    pallas_call x2, Pallas kernels, project(): pl.pallas_call(lambda *refs: project_kernel(len(rows), *refs), out_shape=...  14 us
    all_to_all x2, waiting for transfers between devices, across_chips(): lax.all_to_all(chunks, 'dp', split_axis=0, concat_axis=0, axis_index_grou...  10 us
    ppermute x6, waiting for transfers between devices, to_other_chips(): moved.append(lax.ppermute(chunks[turn], 'dp', pairs))  9.89 us
    all_to_all x2, starting transfers between devices, across_chips(): lax.all_to_all(chunks, 'dp', split_axis=0, concat_axis=0, axis_index_grou...  8.13 us
    ppermute x6, starting transfers between devices, to_other_chips(): moved.append(lax.ppermute(chunks[turn], 'dp', pairs))  7.1 us
    all_to_all x1, starting transfers between devices, shards(): lax.all_to_all(packed, 'tensor', split_axis=0, concat_axis=0, tiled=True)  6.74 us
  transfers between devices with their start and end apart: 16, of which 7 were waited for; matrix products, arithmetic and copies ran while one was open for 7% of the time, Pallas kernels for 23%

profile of v3, /device:TPU:8, one launch (start us, length us, event | category | flops | bytes accessed | tf_op | source)
XLA Modules:
  0.0 181.5 jit_solution(2908721267223617359)
XLA Ops:
  0.7 3.1 %convolution_convert_fusion.5 = bf16[128,16,256]{2,0,1:T(8,128)(2,1)S(1)} fusion(bf16[16,512,256]{2,1,0:T(8,128)(2,1)} %param.16, bf16[128,576]{0,1:T(8,128)(2,1)} %param.15), kind=kOutput, calls=%fused_computation.7 | convolution fusion | flops 537395200 | bytes 5373952 | tf_op jit(solution)/shard_map/tc,hcd->thd/dot_general | solution.py:532
  4.0 1.7 shard_map.156
  6.4 1.4 fusion.5
  7.8 2.1 %convolution_convert_fusion.6 = bf16[16,128,128]{2,1,0:T(8,128)(2,1)S(1)} fusion(bf16[128,16,256]{2,0,1:T(8,128)(2,1)S(1)} %convolution_convert_fusion.5, f32[16,128]{1,0:T(8,128)S(1)} %fusion.30, f32[16,128,128]{1,2,0:T(8,128)} %fusion.5), kind=kOutput, calls=%fused_computation.13 | convolution fusion | flops 68159616 | bytes 3153920 | tf_op jit(solution)/shard_map/hts,shd->thd/dot_general | solution.py:543
  9.9 1.4 convolution_convert_fusion.refs_3_
  11.3 3.7 %all-to-all-start = ((bf16[4,64,2048]{2,1,0:T(8,128)(2,1)}), bf16[4,64,2048]{2,1,0:T(8,128)(2,1)S(1)}, u32[]{:S(2)}, u32[]{:S(2)}) async-start(bf16[4,64,2048]{2,1,0:T(8,128)(2,1)} %bitcast.8), calls=%async_computation | async-start | bytes 2097152 | tf_op jit(solution)/shard_map/all_to_all | solution.py:559
  17.0 14.1 %shard_map.157.refs_4_.refs_3_ = bf16[128,7168]{1,0:T(8,128)(2,1)} custom-call(f32[128,128]{1,0:T(8,128)} %get-tuple-element.38.refs_0_.refs_1_, f32[128,128]{1,0:T(8,128)} %get-tuple-element.38.refs_0_.refs_1_, bf16[256,7168]{1,0:T(8,128)(2,1)} %bitcast.70, bf16[256,2048]{1,0:T(8,128)(2,1)} %convolution_convert_fusion.refs_3_, ...), custom_call_target="tpu_custom_call" | custom-call | flops 16000000000 | bytes 3670016 | tf_op jit(solution)/shard_map/pallas_call | solution.py:154
  32.1 7.1 %shard_map.158.refs_4_ = bf16[4,64,1792]{2,1,0:T(8,128)(2,1)} custom-call(s32[1]{0:T(128)} %bitcast.3.refs_0_, bf16[2048,896]{1,0:T(8,128)(2,1)} %refs_1_.3, bf16[2048,896]{1,0:T(8,128)(2,1)} %collective-permute-done.refs_2_, bf16[4,64,2048]{2,1,0:T(8,128)(2,1)} %copy-done.1, bf16[128,7168]{1,0:T(8,128)(2,1)} %shard_map.157.refs_4_.refs_3_), custom_call_target="tpu_custom_call" | custom-call | flops 1879048192 | bytes 9306112 | tf_op jit(solution)/shard_map/pallas_call | solution.py:249
  39.1 4.4 %all-to-all-start.1 = ((bf16[4,64,1792]{2,1,0:T(8,128)(2,1)}), bf16[4,64,1792]{2,1,0:T(8,128)(2,1)}, u32[]{:S(2)}, u32[]{:S(2)}) async-start(bf16[4,64,1792]{2,1,0:T(8,128)(2,1)} %shard_map.158.refs_4_), calls=%async_computation.1 | async-start | bytes 1835008 | tf_op jit(solution)/shard_map/all_to_all | solution.py:559
  43.5 2.1 %collective-permute-start.1 = (bf16[64,2048]{1,0:T(8,128)(2,1)S(1)}, bf16[64,2048]{1,0:T(8,128)(2,1)S(1)}, u32[]{:S(2)}, u32[]{:S(2)}) collective-permute-start(bf16[64,2048]{1,0:T(8,128)(2,1)S(1)} %copy-done.5), channel_id=1, source_target_pairs={{0,8},{4,12},{8,0},{12,4},{16,24},{20,28},{24,16},{28,20},{1,9},{5... | collective-permute-start | bytes 786440 | tf_op jit(solution)/shard_map/ppermute | solution.py:569
  45.6 1.5 collective-permute-start.2
  47.2 10.0 %all-to-all-done.1 = bf16[4,64,1792]{2,1,0:T(8,128)(2,1)} async-done(((bf16[4,64,1792]{2,1,0:T(8,128)(2,1)}), bf16[4,64,1792]{2,1,0:T(8,128)(2,1)}, u32[]{:S(2)}, u32[]{:S(2)}) %all-to-all-start.1) | async-done | bytes 917536 | tf_op jit(solution)/shard_map/all_to_all | solution.py:559
  57.2 5.3 %all-to-all-start.2 = ((bf16[4,1,64,1792]{3,2,1,0:T(8,128)(2,1)}), bf16[4,1,64,1792]{3,2,1,0:T(8,128)(2,1)S(1)}, u32[]{:S(2)}, u32[]{:S(2)}) async-start(bf16[4,1,64,1792]{3,2,1,0:T(8,128)(2,1)} %bitcast.15), calls=%async_computation.2 | async-start | bytes 1835008 | tf_op jit(solution)/shard_map/all_to_all | solution.py:592
  62.5 14.5 %shard_map.159.rest_0_.refs_7_.refs_1_ = bf16[256,7168]{1,0:T(8,128)(2,1)} custom-call(f32[128,128]{1,0:T(8,128)} %get-tuple-element.39.refs_0_.refs_1_, f32[128,128]{1,0:T(8,128)} %get-tuple-element.39.refs_0_.refs_1_, bf16[256,7168]{1,0:T(8,128)(2,1)} %bitcast.71, bf16[128,7168]{1,0:T(8,128)(2,1)} %shard_map.157.refs_4_.refs_3_, ...), custom_call_target="tpu_custom_call" | custom-call | flops 16000000000 | bytes 3670016 | tf_op jit(solution)/shard_map/pallas_call | solution.py:154
  77.1 3.9 %all-to-all-done.2.arrived = bf16[4,1,64,1792]{3,2,1,0:T(8,128)(2,1)S(1)} async-done(((bf16[4,1,64,1792]{3,2,1,0:T(8,128)(2,1)}), bf16[4,1,64,1792]{3,2,1,0:T(8,128)(2,1)S(1)}, u32[]{:S(2)}, u32[]{:S(2)}) %all-to-all-start.2) | async-done | bytes 917536 | tf_op jit(solution)/shard_map/all_to_all | solution.py:592
  82.0 2.4 %shard_map.160 = (bf16[64,1792]{1,0:T(8,128)(2,1)}, bf16[64,1792]{1,0:T(8,128)(2,1)}) custom-call(bf16[4,1,64,1792]{3,2,1,0:T(8,128)(2,1)} %copy-done.2, bf16[64,128]{1,0:T(8,128)(2,1)} %get-tuple-element.23.order, bf16[128,1792]{1,0:T(8,128)(2,1)} %residual.1, bf16[64,64]{1,0:T(8,128)(2,1)} %get-tuple-element.24.pick, ...), custom_call_target="tpu_custom_call" | custom-call | flops 100000000 | bytes 917504 | tf_op jit(solution)/shard_map/pallas_call | solution.py:288
  84.4 3.4 %all-to-all-start.3 = ((bf16[8,8,1792]{2,1,0:T(8,128)(2,1)}), bf16[8,8,1792]{2,1,0:T(8,128)(2,1)S(1)}, u32[]{:S(2)}, u32[]{:S(2)}) async-start(bf16[8,8,1792]{2,1,0:T(8,128)(2,1)} %bitcast.63), calls=%async_computation.3 | async-start | bytes 458752 | tf_op jit(solution)/shard_map/all_to_all | solution.py:642
  89.9 6.9 %shard_map.161 = (bf16[64,1792]{1,0:T(8,128)(2,1)}, bf16[64,1792]{1,0:T(8,128)(2,1)}, bf16[64,1792]{1,0:T(8,128)(2,1)}, bf16[64,1792]{1,0:T(8,128)(2,1)}) custom-call(s32[1]{0:T(128)} %bitcast.3.refs_0_, bf16[2048,896]{1,0:T(8,128)(2,1)} %refs_1_.3, bf16[2048,896]{1,0:T(8,128)(2,1)} %collective-permute-done.refs_2_, ...), custom_call_target="tpu_custom_call" | custom-call | flops 1879048192 | bytes 9306112 | tf_op jit(solution)/shard_map/pallas_call | solution.py:249
  97.5 5.2 %shard_map.163 = bf16[4,64,640]{2,1,0:T(8,128)(2,1)} custom-call(bf16[64,1792]{1,0:T(8,128)(2,1)} %bitcast.64, bf16[1,1792]{1,0:T(2,128)(2,1)} %broadcast_in_dim.78.gain, bf16[1792,1024]{1,0:T(8,128)(2,1)} %bitcast.58, bf16[1792,1024]{1,0:T(8,128)(2,1)} %bitcast.59, bf16[64,1792]{1,0:T(8,128)(2,1)} %get-tuple-element.26.refs_1_.rest_0_, ...), custom_call_target="tpu_custom_call" | custom-call | flops 469762048 | bytes 7340032 | tf_op jit(solution)/shard_map/pallas_call | solution.py:374
  102.7 6.7 %all-to-all-start.4 = ((bf16[4,64,640]{2,1,0:T(8,128)(2,1)}), bf16[4,64,640]{2,1,0:T(8,128)(2,1)S(1)}, u32[]{:S(2)}, u32[]{:S(2)}) async-start(bf16[4,64,640]{2,1,0:T(8,128)(2,1)} %shard_map.163), calls=%async_computation.4 | async-start | bytes 655360 | tf_op jit(solution)/shard_map/all_to_all | solution.py:653
  109.5 1.9 %collective-permute-start.4 = (bf16[64,1792]{1,0:T(8,128)(2,1)S(1)}, bf16[64,1792]{1,0:T(8,128)(2,1)S(1)}, u32[]{:S(2)}, u32[]{:S(2)}) collective-permute-start(bf16[64,1792]{1,0:T(8,128)(2,1)S(1)} %copy-done.15), channel_id=1, source_target_pairs={{0,8},{4,12},{8,0},{12,4},{16,24},{20,28},{24,16},{28,20},{1,9},{5... | collective-permute-start | bytes 688136 | tf_op jit(solution)/shard_map/ppermute | solution.py:569
  111.4 1.5 collective-permute-start.5
  113.5 4.4 %collective-permute-done.4.refs_2_ = bf16[64,1792]{1,0:T(8,128)(2,1)S(1)} collective-permute-done((bf16[64,1792]{1,0:T(8,128)(2,1)S(1)}, bf16[64,1792]{1,0:T(8,128)(2,1)S(1)}, u32[]{:S(2)}, u32[]{:S(2)}) %collective-permute-start.4) | collective-permute-done | bytes 229408 | tf_op jit(solution)/shard_map/ppermute | solution.py:569
  117.9 5.4 %collective-permute-done.5.refs_3_ = bf16[64,1792]{1,0:T(8,128)(2,1)S(1)} collective-permute-done((bf16[64,1792]{1,0:T(8,128)(2,1)S(1)}, bf16[64,1792]{1,0:T(8,128)(2,1)S(1)}, u32[]{:S(2)}, u32[]{:S(2)}) %collective-permute-start.5) | collective-permute-done | bytes 229408 | tf_op jit(solution)/shard_map/ppermute | solution.py:569
  124.7 2.4 %shard_map.162 = (bf16[64,1792]{1,0:T(8,128)(2,1)}, bf16[64,1792]{1,0:T(8,128)(2,1)}, bf16[64,1792]{1,0:T(8,128)(2,1)}, bf16[64,1792]{1,0:T(8,128)(2,1)}) custom-call(s32[4]{0:T(128)} %fusion.22.refs_0_, bf16[64,1792]{1,0:T(8,128)(2,1)} %get-tuple-element.26.refs_1_.rest_0_, bf16[64,1792]{1,0:T(8,128)(2,1)} %copy-done.16, bf16[64,1792]{1,0:T(8,128)(2,1)} %copy-done.18, ...), custom_call_target="tpu_custom_call" | custom-call | bytes 1835008 | tf_op jit(solution)/shard_map/pallas_call | solution.py:315
  127.9 4.5 %shard_map.164 = (bf16[64,7168]{1,0:T(8,128)(2,1)}, f32[256,128]{1,0:T(8,128)}) custom-call(bf16[4,64,640]{2,1,0:T(8,128)(2,1)} %copy-done.4, bf16[256,7168]{1,0:T(8,128)(2,1)} %shard_map.159.rest_0_.refs_7_.refs_1_, bf16[64,1792]{1,0:T(8,128)(2,1)} %get-tuple-element.31.refs_2_, bf16[64,1792]{1,0:T(8,128)(2,1)} %get-tuple-element.32.refs_3_, ...), custom_call_target="tpu_custom_call" | custom-call | flops 234881024 | bytes 3670016 | tf_op jit(solution)/shard_map/pallas_call | solution.py:439
  132.4 4.9 %all-to-all-start.5 = ((bf16[32,8,1792]{2,1,0:T(8,128)(2,1)}), bf16[32,8,1792]{2,1,0:T(8,128)(2,1)S(1)}, u32[]{:S(2)}, u32[]{:S(2)}) async-start(bf16[32,8,1792]{2,1,0:T(8,128)(2,1)} %bitcast.62), calls=%async_computation.5 | async-start | bytes 1835008 | tf_op jit(solution)/shard_map/all_to_all | solution.py:673
  137.3 1.5 collective-permute-start.7
  140.0 1.8 %collective-permute-start.9 = (bf16[64,1792]{1,0:T(8,128)(2,1)S(1)}, bf16[64,1792]{1,0:T(8,128)(2,1)S(1)}, u32[]{:S(2)}, u32[]{:S(2)}) collective-permute-start(bf16[64,1792]{1,0:T(8,128)(2,1)S(1)} %copy-done.17), channel_id=1, source_target_pairs={{0,3},{1,0},{2,1},{3,2},{4,7},{5,4},{6,5},{7,6},{8,11},{9,8},{10,9... | collective-permute-start | bytes 688136 | tf_op jit(solution)/shard_map/ppermute | solution.py:585
  142.0 30.8 %collective-permute-done.7 = bf16[64,1792]{1,0:T(8,128)(2,1)S(1)} collective-permute-done((bf16[64,1792]{1,0:T(8,128)(2,1)}, bf16[64,1792]{1,0:T(8,128)(2,1)S(1)}, u32[]{:S(2)}, u32[]{:S(2)}) %collective-permute-start.7) | collective-permute-done | bytes 229408 | tf_op jit(solution)/shard_map/ppermute | solution.py:585
  172.8 4.5 %collective-permute-done.8 = bf16[64,1792]{1,0:T(8,128)(2,1)S(1)} collective-permute-done((bf16[64,1792]{1,0:T(8,128)(2,1)S(1)}, bf16[64,1792]{1,0:T(8,128)(2,1)S(1)}, u32[]{:S(2)}, u32[]{:S(2)}) %collective-permute-start.8) | collective-permute-done | bytes 229408 | tf_op jit(solution)/shard_map/ppermute | solution.py:585
  177.3 1.9 %collective-permute-done.9 = bf16[64,1792]{1,0:T(8,128)(2,1)S(1)} collective-permute-done((bf16[64,1792]{1,0:T(8,128)(2,1)S(1)}, bf16[64,1792]{1,0:T(8,128)(2,1)S(1)}, u32[]{:S(2)}, u32[]{:S(2)}) %collective-permute-start.9) | collective-permute-done | bytes 229408 | tf_op jit(solution)/shard_map/ppermute | solution.py:585
  (84 shorter events, 14.0 us)
Async XLA Ops:
  0.6 5.2 %copy-start = (bf16[128,16,192]{0,2,1:T(8,128)(2,1)S(1)}, bf16[128,16,192]{0,2,1:T(8,128)(2,1)}, u32[]{:S(2)}) copy-start(bf16[128,16,192]{0,2,1:T(8,128)(2,1)} %param.14) | copy-start | bytes 2359300
  0.7 30.4 %collective-permute-start = (bf16[2048,896]{1,0:T(8,128)(2,1)}, bf16[2048,896]{1,0:T(8,128)(2,1)}, u32[]{:S(2)}, u32[]{:S(2)}) collective-permute-start(bf16[2048,896]{1,0:T(8,128)(2,1)} %refs_1_.3), channel_id=1, source_target_pairs={{0,4},{4,0},{8,12},{12,8},{16,20},{20,16},{24,28},{28,24},{1,5},{5... | collective-permute-start | bytes 11010056 | tf_op jit(solution)/shard_map/ppermute | solution.py:617
  6.4 3.5 %copy-start.22 = (bf16[256,128]{1,0:T(8,128)(2,1)S(1)}, bf16[256,128]{1,0:T(8,128)(2,1)}, u32[]{:S(2)}) copy-start(bf16[256,128]{1,0:T(8,128)(2,1)} %get-tuple-element.22) | copy-start | bytes 196612
  7.8 7.3 %copy-start.8 = (f32[1,256,128]{2,1,0:T(8,128)S(1)}, f32[1,256,128]{2,1,0:T(8,128)}, u32[]{:S(2)}) copy-start(f32[1,256,128]{2,1,0:T(8,128)} %param.25) | copy-start | bytes 393220
  7.8 8.2 %copy-start.21 = (bf16[128,128]{1,0:T(8,128)(2,1)S(1)}, bf16[128,128]{1,0:T(8,128)(2,1)}, u32[]{:S(2)}) copy-start(bf16[128,128]{1,0:T(8,128)(2,1)} %get-tuple-element.21) | copy-start | bytes 98308
  11.3 19.8 %all-to-all-start = ((bf16[4,64,2048]{2,1,0:T(8,128)(2,1)}), bf16[4,64,2048]{2,1,0:T(8,128)(2,1)S(1)}, u32[]{:S(2)}, u32[]{:S(2)}) async-start(bf16[4,64,2048]{2,1,0:T(8,128)(2,1)} %bitcast.8), calls=%async_computation | async-start | bytes 2097152 | tf_op jit(solution)/shard_map/all_to_all | solution.py:559
  32.1 11.5 %copy-start.5 = (bf16[64,2048]{1,0:T(8,128)(2,1)S(1)}, bf16[64,2048]{1,0:T(8,128)(2,1)}, u32[]{:S(2)}) copy-start(bf16[64,2048]{1,0:T(8,128)(2,1)} %convolution_convert_fusion.4.refs_4_.refs_3_) | copy-start | bytes 786436
  39.1 18.1 %all-to-all-start.1 = ((bf16[4,64,1792]{2,1,0:T(8,128)(2,1)}), bf16[4,64,1792]{2,1,0:T(8,128)(2,1)}, u32[]{:S(2)}, u32[]{:S(2)}) async-start(bf16[4,64,1792]{2,1,0:T(8,128)(2,1)} %shard_map.158.refs_4_), calls=%async_computation.1 | async-start | bytes 1835008 | tf_op jit(solution)/shard_map/all_to_all | solution.py:559
  43.5 44.8 %collective-permute-start.1 = (bf16[64,2048]{1,0:T(8,128)(2,1)S(1)}, bf16[64,2048]{1,0:T(8,128)(2,1)S(1)}, u32[]{:S(2)}, u32[]{:S(2)}) collective-permute-start(bf16[64,2048]{1,0:T(8,128)(2,1)S(1)} %copy-done.5), channel_id=1, source_target_pairs={{0,8},{4,12},{8,0},{12,4},{16,24},{20,28},{24,16},{28,20},{1,9},{5... | collective-permute-start | bytes 786440 | tf_op jit(solution)/shard_map/ppermute | solution.py:569
  45.6 42.8 %collective-permute-start.2 = (bf16[64,2048]{1,0:T(8,128)(2,1)S(1)}, bf16[64,2048]{1,0:T(8,128)(2,1)S(1)}, u32[]{:S(2)}, u32[]{:S(2)}) collective-permute-start(bf16[64,2048]{1,0:T(8,128)(2,1)S(1)} %copy-done.5), channel_id=1, source_target_pairs={{0,16},{4,20},{8,24},{12,28},{16,0},{20,4},{24,8},{28,12},{1,17},{... | collective-permute-start | bytes 786440 | tf_op jit(solution)/shard_map/ppermute | solution.py:569
  47.1 41.3 %collective-permute-start.3 = (bf16[64,2048]{1,0:T(8,128)(2,1)S(1)}, bf16[64,2048]{1,0:T(8,128)(2,1)S(1)}, u32[]{:S(2)}, u32[]{:S(2)}) collective-permute-start(bf16[64,2048]{1,0:T(8,128)(2,1)S(1)} %copy-done.5), channel_id=1, source_target_pairs={{0,24},{4,28},{8,16},{12,20},{16,8},{20,12},{24,0},{28,4},{1,25},{... | collective-permute-start | bytes 786440 | tf_op jit(solution)/shard_map/ppermute | solution.py:569
  57.2 23.8 %all-to-all-start.2 = ((bf16[4,1,64,1792]{3,2,1,0:T(8,128)(2,1)}), bf16[4,1,64,1792]{3,2,1,0:T(8,128)(2,1)S(1)}, u32[]{:S(2)}, u32[]{:S(2)}) async-start(bf16[4,1,64,1792]{3,2,1,0:T(8,128)(2,1)} %bitcast.15), calls=%async_computation.2 | async-start | bytes 1835008 | tf_op jit(solution)/shard_map/all_to_all | solution.py:592
  77.1 10.7 %copy-start.24 = (bf16[1792]{0:T(1024)(128)(2,1)S(1)}, bf16[1792]{0:T(1024)(128)(2,1)}, u32[]{:S(2)}) copy-start(bf16[1792]{0:T(1024)(128)(2,1)} %param.18) | copy-start | bytes 10756
  84.4 12.4 %all-to-all-start.3 = ((bf16[8,8,1792]{2,1,0:T(8,128)(2,1)}), bf16[8,8,1792]{2,1,0:T(8,128)(2,1)S(1)}, u32[]{:S(2)}, u32[]{:S(2)}) async-start(bf16[8,8,1792]{2,1,0:T(8,128)(2,1)} %bitcast.63), calls=%async_computation.3 | async-start | bytes 458752 | tf_op jit(solution)/shard_map/all_to_all | solution.py:642
  97.5 12.0 %copy-start.15 = (bf16[64,1792]{1,0:T(8,128)(2,1)S(1)}, bf16[64,1792]{1,0:T(8,128)(2,1)}, u32[]{:S(2)}) copy-start(bf16[64,1792]{1,0:T(8,128)(2,1)} %get-tuple-element.27.rest_1_) | copy-start | bytes 688132
  97.5 13.8 %copy-start.14 = (bf16[64,1792]{1,0:T(8,128)(2,1)S(1)}, bf16[64,1792]{1,0:T(8,128)(2,1)}, u32[]{:S(2)}) copy-start(bf16[64,1792]{1,0:T(8,128)(2,1)} %get-tuple-element.28.rest_2_) | copy-start | bytes 688132
  97.5 15.3 %copy-start.13 = (bf16[64,1792]{1,0:T(8,128)(2,1)S(1)}, bf16[64,1792]{1,0:T(8,128)(2,1)}, u32[]{:S(2)}) copy-start(bf16[64,1792]{1,0:T(8,128)(2,1)} %get-tuple-element.29.rest_3_) | copy-start | bytes 688132
  102.7 24.4 %all-to-all-start.4 = ((bf16[4,64,640]{2,1,0:T(8,128)(2,1)}), bf16[4,64,640]{2,1,0:T(8,128)(2,1)S(1)}, u32[]{:S(2)}, u32[]{:S(2)}) async-start(bf16[4,64,640]{2,1,0:T(8,128)(2,1)} %shard_map.163), calls=%async_computation.4 | async-start | bytes 655360 | tf_op jit(solution)/shard_map/all_to_all | solution.py:653
  109.5 8.5 %collective-permute-start.4 = (bf16[64,1792]{1,0:T(8,128)(2,1)S(1)}, bf16[64,1792]{1,0:T(8,128)(2,1)S(1)}, u32[]{:S(2)}, u32[]{:S(2)}) collective-permute-start(bf16[64,1792]{1,0:T(8,128)(2,1)S(1)} %copy-done.15), channel_id=1, source_target_pairs={{0,8},{4,12},{8,0},{12,4},{16,24},{20,28},{24,16},{28,20},{1,9},{5... | collective-permute-start | bytes 688136 | tf_op jit(solution)/shard_map/ppermute | solution.py:569
  111.4 12.0 %collective-permute-start.5 = (bf16[64,1792]{1,0:T(8,128)(2,1)S(1)}, bf16[64,1792]{1,0:T(8,128)(2,1)S(1)}, u32[]{:S(2)}, u32[]{:S(2)}) collective-permute-start(bf16[64,1792]{1,0:T(8,128)(2,1)S(1)} %copy-done.14), channel_id=1, source_target_pairs={{0,16},{4,20},{8,24},{12,28},{16,0},{20,4},{24,8},{28,12},{1,17},{... | collective-permute-start | bytes 688136 | tf_op jit(solution)/shard_map/ppermute | solution.py:569
  112.9 10.5 %collective-permute-start.6 = (bf16[64,1792]{1,0:T(8,128)(2,1)S(1)}, bf16[64,1792]{1,0:T(8,128)(2,1)S(1)}, u32[]{:S(2)}, u32[]{:S(2)}) collective-permute-start(bf16[64,1792]{1,0:T(8,128)(2,1)S(1)} %copy-done.13), channel_id=1, source_target_pairs={{0,24},{4,28},{8,16},{12,20},{16,8},{20,12},{24,0},{28,4},{1,25},{... | collective-permute-start | bytes 688136 | tf_op jit(solution)/shard_map/ppermute | solution.py:569
  113.5 28.3 %copy-start.3 = (bf16[128,1792]{1,0:T(8,128)(2,1)S(1)}, bf16[128,1792]{1,0:T(8,128)(2,1)}, u32[]{:S(2)}) copy-start(bf16[128,1792]{1,0:T(8,128)(2,1)} %residual.1) | copy-start | bytes 1376260
  117.9 5.5 %copy-start.16 = (bf16[64,1792]{1,0:T(8,128)(2,1)}, bf16[64,1792]{1,0:T(8,128)(2,1)S(1)}, u32[]{:S(2)}) copy-start(bf16[64,1792]{1,0:T(8,128)(2,1)S(1)} %collective-permute-done.4.refs_2_) | copy-start | bytes 688132
  127.1 11.7 %copy-start.19 = (bf16[64,1792]{1,0:T(8,128)(2,1)S(1)}, bf16[64,1792]{1,0:T(8,128)(2,1)}, u32[]{:S(2)}) copy-start(bf16[64,1792]{1,0:T(8,128)(2,1)} %get-tuple-element.33.refs_4_) | copy-start | bytes 688132
  127.1 12.9 %copy-start.17 = (bf16[64,1792]{1,0:T(8,128)(2,1)S(1)}, bf16[64,1792]{1,0:T(8,128)(2,1)}, u32[]{:S(2)}) copy-start(bf16[64,1792]{1,0:T(8,128)(2,1)} %get-tuple-element.34.refs_5_) | copy-start | bytes 688132
  127.9 51.3 %copy-start.6 = (bf16[64,1792]{1,0:T(8,128)(2,1)S(1)}, bf16[64,1792]{1,0:T(8,128)(2,1)}, u32[]{:S(2)}) copy-start(bf16[64,1792]{1,0:T(8,128)(2,1)} %get-tuple-element.31.refs_2_) | copy-start | bytes 688132
  127.9 51.5 %copy-start.12 = (bf16[64,1792]{1,0:T(8,128)(2,1)S(1)}, bf16[64,1792]{1,0:T(8,128)(2,1)}, u32[]{:S(2)}) copy-start(bf16[64,1792]{1,0:T(8,128)(2,1)} %get-tuple-element.25) | copy-start | bytes 688132
  132.4 48.0 %copy-start.23 = (bf16[64,128]{1,0:T(8,128)(2,1)S(1)}, bf16[64,128]{1,0:T(8,128)(2,1)}, u32[]{:S(2)}) copy-start(bf16[64,128]{1,0:T(8,128)(2,1)} %get-tuple-element.35) | copy-start | bytes 49156
  132.4 48.0 %all-to-all-start.5 = ((bf16[32,8,1792]{2,1,0:T(8,128)(2,1)}), bf16[32,8,1792]{2,1,0:T(8,128)(2,1)S(1)}, u32[]{:S(2)}, u32[]{:S(2)}) async-start(bf16[32,8,1792]{2,1,0:T(8,128)(2,1)} %bitcast.62), calls=%async_computation.5 | async-start | bytes 1835008 | tf_op jit(solution)/shard_map/all_to_all | solution.py:673
  137.3 35.5 %collective-permute-start.7 = (bf16[64,1792]{1,0:T(8,128)(2,1)}, bf16[64,1792]{1,0:T(8,128)(2,1)S(1)}, u32[]{:S(2)}, u32[]{:S(2)}) collective-permute-start(bf16[64,1792]{1,0:T(8,128)(2,1)} %get-tuple-element.32.refs_3_), channel_id=1, source_target_pairs={{0,1},{1,2},{2,3},{3,0},{4,5},{5,6},{6,7},{7,4},{8,9},{9,10},{10,1... | collective-permute-start | bytes 688136 | tf_op jit(solution)/shard_map/ppermute | solution.py:585
  138.8 38.4 %collective-permute-start.8 = (bf16[64,1792]{1,0:T(8,128)(2,1)S(1)}, bf16[64,1792]{1,0:T(8,128)(2,1)S(1)}, u32[]{:S(2)}, u32[]{:S(2)}) collective-permute-start(bf16[64,1792]{1,0:T(8,128)(2,1)S(1)} %copy-done.19), channel_id=1, source_target_pairs={{0,2},{1,3},{2,0},{3,1},{4,6},{5,7},{6,4},{7,5},{8,10},{9,11},{10,... | collective-permute-start | bytes 688136 | tf_op jit(solution)/shard_map/ppermute | solution.py:585
  140.0 39.2 %collective-permute-start.9 = (bf16[64,1792]{1,0:T(8,128)(2,1)S(1)}, bf16[64,1792]{1,0:T(8,128)(2,1)S(1)}, u32[]{:S(2)}, u32[]{:S(2)}) collective-permute-start(bf16[64,1792]{1,0:T(8,128)(2,1)S(1)} %copy-done.17), channel_id=1, source_target_pairs={{0,3},{1,0},{2,1},{3,2},{4,7},{5,4},{6,5},{7,6},{8,11},{9,8},{10,9... | collective-permute-start | bytes 688136 | tf_op jit(solution)/shard_map/ppermute | solution.py:585
  (10 other events, 10.2 us)

commit v4 on v3

--- a/solution.py
+++ b/solution.py
@@ -637,11 +637,13 @@
         later = project(core, later, out_proj, partner, partly[0])
     quantized = partly[0]
     front, outgoing = make_front(
-        across_ranks(arrived, ranks), order_first, residual_in, pick, quantized
+        across_ranks(arrived, ranks), order_first, residual_in, pick, quantized, *later
     )
     incoming = lax.all_to_all(
         outgoing.reshape(owners, CAP, -1), "dp", split_axis=0, concat_axis=0, tiled=True
     )
+    if later:
+        later = in_order_of_ranks(to_other_chips(later), outgoing)
     packed = gate_and_up(
         incoming.reshape(owners * CAP, -1),
         norm_gain[None, :],
@@ -651,9 +653,7 @@
         *later,
     )
     packed = lax.all_to_all(packed, "tensor", split_axis=0, concat_axis=0, tiled=True)
-    if later:
-        later = in_order_of_ranks(to_other_chips(later), outgoing)
-    expert_part, gram = expert_outputs(packed, quantized, model_cols * ranks, *later)
+    expert_part, gram = expert_outputs(packed, quantized, model_cols * ranks)
     if later:
         later = to_other_ranks(later)
     ordered_out = front

time: 183 us -> 176 us (0.962)
  blocking collectives: 0 us -> 13.5 us
  waiting for transfers between devices: 61.1 us -> 48.8 us
  starting transfers between devices: 40.1 us -> 33.4 us
    all_to_all x0 -> x1, blocking collectives: none -> 13.5 us  [shards(): lax.all_to_all(packed, 'tensor', split_axis=0, concat_axis=0, tiled=True)]
    ppermute x6, waiting for transfers between devices: 9.89 us -> 0.56 us  [to_other_chips(): moved.append(lax.ppermute(chunks[turn], 'dp', pairs))]
    all_to_all x1 -> x0, starting transfers between devices: 6.74 us -> none  [shards(): lax.all_to_all(packed, 'tensor', split_axis=0, concat_axis=0, tiled=True)]
    all_to_all x1, waiting for transfers between devices: 3.95 us -> 0.01 us  [across_ranks(): lax.all_to_all(chunks, 'tensor', split_axis=0, concat_axis=0, tiled=True)]
    unnamed x50 -> x44, local copies, waits for them, and re-layouts: 6.19 us -> 5.48 us
  transfers between devices with their start and end apart: 16 -> 15, of which waited for: 7 -> 6; matrix products, arithmetic and copies ran while one was open for 7% -> 8% of each run, Pallas kernels for 23% -> 24%
where the time goes in v4:
time: 176 us; the launch traced here: 175 us
  Pallas kernels  58.7 us (33%)
  waiting for transfers between devices  48.8 us (28%)
  starting transfers between devices  33.4 us (19%)
  blocking collectives  13.5 us (8%)
  matrix products  11.9 us (7%)
  local copies, waits for them, and re-layouts  7.07 us (4%)
    ppermute x3, waiting for transfers between devices, to_other_ranks(): moved.append(lax.ppermute(chunks[shift], 'tensor', pairs))  37.2 us
    pallas_call x2, Pallas kernels, quantize_panel(): pl.pallas_call(lambda *refs: quantize_kernel(index * PANEL, len(partly),...  28.6 us
    pallas_call x2, Pallas kernels, project(): pl.pallas_call(lambda *refs: project_kernel(len(rows), *refs), out_shape=...  14 us
    all_to_all x1, blocking collectives, shards(): lax.all_to_all(packed, 'tensor', split_axis=0, concat_axis=0, tiled=True)  13.5 us
    all_to_all x2, waiting for transfers between devices, across_chips(): lax.all_to_all(chunks, 'dp', split_axis=0, concat_axis=0, axis_index_grou...  10 us
    all_to_all x2, starting transfers between devices, across_chips(): lax.all_to_all(chunks, 'dp', split_axis=0, concat_axis=0, axis_index_grou...  8.13 us
    ppermute x6, starting transfers between devices, to_other_chips(): moved.append(lax.ppermute(chunks[turn], 'dp', pairs))  7.19 us
    unnamed x44, local copies, waits for them, and re-layouts  5.48 us
  transfers between devices with their start and end apart: 15, of which 6 were waited for; matrix products, arithmetic and copies ran while one was open for 8% of the time, Pallas kernels for 24%

profile of v4, /device:TPU:8, one launch (start us, length us, event | category | flops | bytes accessed | tf_op | source)
XLA Modules:
  0.0 175.3 jit_solution(2488809147023055686)
XLA Ops:
  0.7 3.1 %convolution_convert_fusion.5 = bf16[128,16,256]{2,0,1:T(8,128)(2,1)S(1)} fusion(bf16[16,512,256]{2,1,0:T(8,128)(2,1)} %param.16, bf16[128,576]{0,1:T(8,128)(2,1)} %param.15), kind=kOutput, calls=%fused_computation.7 | convolution fusion | flops 537395200 | bytes 5373952 | tf_op jit(solution)/shard_map/tc,hcd->thd/dot_general | solution.py:532
  4.0 1.7 shard_map.156
  6.4 1.4 fusion.5
  7.8 2.1 %convolution_convert_fusion.6 = bf16[16,128,128]{2,1,0:T(8,128)(2,1)S(1)} fusion(bf16[128,16,256]{2,0,1:T(8,128)(2,1)S(1)} %convolution_convert_fusion.5, f32[16,128]{1,0:T(8,128)S(1)} %fusion.30, f32[16,128,128]{1,2,0:T(8,128)} %fusion.5), kind=kOutput, calls=%fused_computation.13 | convolution fusion | flops 68159616 | bytes 3153920 | tf_op jit(solution)/shard_map/hts,shd->thd/dot_general | solution.py:543
  9.9 1.4 convolution_convert_fusion.refs_3_
  11.3 3.7 %all-to-all-start = ((bf16[4,64,2048]{2,1,0:T(8,128)(2,1)}), bf16[4,64,2048]{2,1,0:T(8,128)(2,1)S(1)}, u32[]{:S(2)}, u32[]{:S(2)}) async-start(bf16[4,64,2048]{2,1,0:T(8,128)(2,1)} %bitcast.8), calls=%async_computation | async-start | bytes 2097152 | tf_op jit(solution)/shard_map/all_to_all | solution.py:559
  17.0 14.1 %shard_map.157.refs_4_.refs_3_ = bf16[128,7168]{1,0:T(8,128)(2,1)} custom-call(f32[128,128]{1,0:T(8,128)} %get-tuple-element.38.refs_0_.refs_1_, f32[128,128]{1,0:T(8,128)} %get-tuple-element.38.refs_0_.refs_1_, bf16[256,7168]{1,0:T(8,128)(2,1)} %bitcast.70, bf16[256,2048]{1,0:T(8,128)(2,1)} %convolution_convert_fusion.refs_3_, ...), custom_call_target="tpu_custom_call" | custom-call | flops 16000000000 | bytes 3670016 | tf_op jit(solution)/shard_map/pallas_call | solution.py:154
  32.1 7.0 %shard_map.158.refs_4_ = bf16[4,64,1792]{2,1,0:T(8,128)(2,1)} custom-call(s32[1]{0:T(128)} %bitcast.3.refs_0_, bf16[2048,896]{1,0:T(8,128)(2,1)} %refs_1_.3, bf16[2048,896]{1,0:T(8,128)(2,1)} %collective-permute-done.refs_2_, bf16[4,64,2048]{2,1,0:T(8,128)(2,1)} %copy-done.1, bf16[128,7168]{1,0:T(8,128)(2,1)} %shard_map.157.refs_4_.refs_3_), custom_call_target="tpu_custom_call" | custom-call | flops 1879048192 | bytes 9306112 | tf_op jit(solution)/shard_map/pallas_call | solution.py:249
  39.1 4.4 %all-to-all-start.1 = ((bf16[4,64,1792]{2,1,0:T(8,128)(2,1)}), bf16[4,64,1792]{2,1,0:T(8,128)(2,1)}, u32[]{:S(2)}, u32[]{:S(2)}) async-start(bf16[4,64,1792]{2,1,0:T(8,128)(2,1)} %shard_map.158.refs_4_), calls=%async_computation.1 | async-start | bytes 1835008 | tf_op jit(solution)/shard_map/all_to_all | solution.py:559
  43.5 2.1 %collective-permute-start.1 = (bf16[64,2048]{1,0:T(8,128)(2,1)S(1)}, bf16[64,2048]{1,0:T(8,128)(2,1)S(1)}, u32[]{:S(2)}, u32[]{:S(2)}) collective-permute-start(bf16[64,2048]{1,0:T(8,128)(2,1)S(1)} %copy-done.4), channel_id=1, source_target_pairs={{0,8},{4,12},{8,0},{12,4},{16,24},{20,28},{24,16},{28,20},{1,9},{5... | collective-permute-start | bytes 786440 | tf_op jit(solution)/shard_map/ppermute | solution.py:569
  45.6 1.4 collective-permute-start.2
  47.2 10.0 %all-to-all-done.1 = bf16[4,64,1792]{2,1,0:T(8,128)(2,1)} async-done(((bf16[4,64,1792]{2,1,0:T(8,128)(2,1)}), bf16[4,64,1792]{2,1,0:T(8,128)(2,1)}, u32[]{:S(2)}, u32[]{:S(2)}) %all-to-all-start.1) | async-done | bytes 917536 | tf_op jit(solution)/shard_map/all_to_all | solution.py:559
  57.2 5.3 %all-to-all-start.2 = ((bf16[4,1,64,1792]{3,2,1,0:T(8,128)(2,1)}), bf16[4,1,64,1792]{3,2,1,0:T(8,128)(2,1)S(1)}, u32[]{:S(2)}, u32[]{:S(2)}) async-start(bf16[4,1,64,1792]{3,2,1,0:T(8,128)(2,1)} %bitcast.15), calls=%async_computation.2 | async-start | bytes 1835008 | tf_op jit(solution)/shard_map/all_to_all | solution.py:592
  62.5 14.5 %shard_map.159.refs_7_.rest_0_.refs_1_ = bf16[256,7168]{1,0:T(8,128)(2,1)} custom-call(f32[128,128]{1,0:T(8,128)} %get-tuple-element.39.refs_0_.refs_1_, f32[128,128]{1,0:T(8,128)} %get-tuple-element.39.refs_0_.refs_1_, bf16[256,7168]{1,0:T(8,128)(2,1)} %bitcast.71, bf16[128,7168]{1,0:T(8,128)(2,1)} %shard_map.157.refs_4_.refs_3_, ...), custom_call_target="tpu_custom_call" | custom-call | flops 16000000000 | bytes 3670016 | tf_op jit(solution)/shard_map/pallas_call | solution.py:154
  78.6 6.9 %shard_map.160 = (bf16[64,1792]{1,0:T(8,128)(2,1)}, bf16[64,1792]{1,0:T(8,128)(2,1)}, bf16[64,1792]{1,0:T(8,128)(2,1)}, bf16[64,1792]{1,0:T(8,128)(2,1)}) custom-call(s32[1]{0:T(128)} %bitcast.3.refs_0_, bf16[2048,896]{1,0:T(8,128)(2,1)} %refs_1_.3, bf16[2048,896]{1,0:T(8,128)(2,1)} %collective-permute-done.refs_2_, ...), custom_call_target="tpu_custom_call" | custom-call | flops 1879048192 | bytes 9306112 | tf_op jit(solution)/shard_map/pallas_call | solution.py:249
  85.6 1.5 collective-permute-start.4
  87.6 1.5 collective-permute-start.6
  90.1 2.4 %shard_map.161 = (bf16[64,1792]{1,0:T(8,128)(2,1)}, bf16[64,1792]{1,0:T(8,128)(2,1)}) custom-call(bf16[4,1,64,1792]{3,2,1,0:T(8,128)(2,1)} %copy-done.2, bf16[64,128]{1,0:T(8,128)(2,1)} %get-tuple-element.23.order, bf16[128,1792]{1,0:T(8,128)(2,1)} %residual.1, bf16[64,64]{1,0:T(8,128)(2,1)} %get-tuple-element.24.pick, ...), custom_call_target="tpu_custom_call" | custom-call | flops 100000000 | bytes 917504 | tf_op jit(solution)/shard_map/pallas_call | solution.py:288
  92.4 3.4 %all-to-all-start.3 = ((bf16[8,8,1792]{2,1,0:T(8,128)(2,1)}), bf16[8,8,1792]{2,1,0:T(8,128)(2,1)S(1)}, u32[]{:S(2)}, u32[]{:S(2)}) async-start(bf16[8,8,1792]{2,1,0:T(8,128)(2,1)} %bitcast.64), calls=%async_computation.3 | async-start | bytes 458752 | tf_op jit(solution)/shard_map/all_to_all | solution.py:642
  98.9 2.4 %shard_map.162 = (bf16[64,1792]{1,0:T(8,128)(2,1)}, bf16[64,1792]{1,0:T(8,128)(2,1)}, bf16[64,1792]{1,0:T(8,128)(2,1)}, bf16[64,1792]{1,0:T(8,128)(2,1)}) custom-call(s32[4]{0:T(128)} %fusion.22.refs_0_, bf16[64,1792]{1,0:T(8,128)(2,1)} %get-tuple-element.25.rest_1_.refs_1_, bf16[64,1792]{1,0:T(8,128)(2,1)} %copy-done.12, bf16[64,1792]{1,0:T(8,128)(2,1)} %copy-done.13, ...), custom_call_target="tpu_custom_call" | custom-call | bytes 1835008 | tf_op jit(solution)/shard_map/pallas_call | solution.py:315
  103.1 5.1 %shard_map.163 = bf16[4,64,640]{2,1,0:T(8,128)(2,1)} custom-call(bf16[64,1792]{1,0:T(8,128)(2,1)} %bitcast.63, bf16[1,1792]{1,0:T(2,128)(2,1)} %broadcast_in_dim.78.gain, bf16[1792,1024]{1,0:T(8,128)(2,1)} %bitcast.58, bf16[1792,1024]{1,0:T(8,128)(2,1)} %bitcast.59, bf16[64,1792]{1,0:T(8,128)(2,1)} %get-tuple-element.31.rest_0_, ...), custom_call_target="tpu_custom_call" | custom-call | flops 469762048 | bytes 7340032 | tf_op jit(solution)/shard_map/pallas_call | solution.py:374
  108.3 13.5 %all_to_all.30.refs_0_ = bf16[4,64,640]{2,1,0:T(8,128)(2,1)} all-to-all(bf16[4,64,640]{2,1,0:T(8,128)(2,1)} %shard_map.163), channel_id=1, replica_groups=mesh['dp'=8,'tensor'=4] {'tensor'}, dimensions={0} | all-to-all | bytes 655360 | tf_op jit(solution)/shard_map/all_to_all | solution.py:655
  121.8 4.5 %shard_map.164 = (bf16[64,7168]{1,0:T(8,128)(2,1)}, f32[256,128]{1,0:T(8,128)}) custom-call(bf16[4,64,640]{2,1,0:T(8,128)(2,1)} %all_to_all.30.refs_0_, bf16[256,7168]{1,0:T(8,128)(2,1)} %shard_map.159.refs_7_.rest_0_.refs_1_), custom_call_target="tpu_custom_call" | custom-call | flops 234881024 | bytes 3670016 | tf_op jit(solution)/shard_map/pallas_call | solution.py:439
  126.3 4.8 %all-to-all-start.5 = ((bf16[32,8,1792]{2,1,0:T(8,128)(2,1)}), bf16[32,8,1792]{2,1,0:T(8,128)(2,1)S(1)}, u32[]{:S(2)}, u32[]{:S(2)}) async-start(bf16[32,8,1792]{2,1,0:T(8,128)(2,1)} %bitcast.62), calls=%async_computation.5 | async-start | bytes 1835008 | tf_op jit(solution)/shard_map/all_to_all | solution.py:673
  131.1 1.5 collective-permute-start.7
  132.6 1.1 collective-permute-start.8
  133.8 1.8 %collective-permute-start.9 = (bf16[64,1792]{1,0:T(8,128)(2,1)S(1)}, bf16[64,1792]{1,0:T(8,128)(2,1)S(1)}, u32[]{:S(2)}, u32[]{:S(2)}) collective-permute-start(bf16[64,1792]{1,0:T(8,128)(2,1)S(1)} %copy-done.15), channel_id=1, source_target_pairs={{0,3},{1,0},{2,1},{3,2},{4,7},{5,4},{6,5},{7,6},{8,11},{9,8},{10,9... | collective-permute-start | bytes 688136 | tf_op jit(solution)/shard_map/ppermute | solution.py:585
  135.8 30.6 %collective-permute-done.7 = bf16[64,1792]{1,0:T(8,128)(2,1)S(1)} collective-permute-done((bf16[64,1792]{1,0:T(8,128)(2,1)S(1)}, bf16[64,1792]{1,0:T(8,128)(2,1)S(1)}, u32[]{:S(2)}, u32[]{:S(2)}) %collective-permute-start.7) | collective-permute-done | bytes 229408 | tf_op jit(solution)/shard_map/ppermute | solution.py:585
  166.5 4.6 %collective-permute-done.8 = bf16[64,1792]{1,0:T(8,128)(2,1)S(1)} collective-permute-done((bf16[64,1792]{1,0:T(8,128)(2,1)S(1)}, bf16[64,1792]{1,0:T(8,128)(2,1)S(1)}, u32[]{:S(2)}, u32[]{:S(2)}) %collective-permute-start.8) | collective-permute-done | bytes 229408 | tf_op jit(solution)/shard_map/ppermute | solution.py:585
  171.0 1.9 %collective-permute-done.9 = bf16[64,1792]{1,0:T(8,128)(2,1)S(1)} collective-permute-done((bf16[64,1792]{1,0:T(8,128)(2,1)S(1)}, bf16[64,1792]{1,0:T(8,128)(2,1)S(1)}, u32[]{:S(2)}, u32[]{:S(2)}) %collective-permute-start.9) | collective-permute-done | bytes 229408 | tf_op jit(solution)/shard_map/ppermute | solution.py:585
  173.1 1.1 convolution_convert_fusion.2
  174.2 1.1 convolution_convert_fusion.1
  (77 shorter events, 12.1 us)
Async XLA Ops:
  0.6 5.2 %copy-start = (bf16[128,16,192]{0,2,1:T(8,128)(2,1)S(1)}, bf16[128,16,192]{0,2,1:T(8,128)(2,1)}, u32[]{:S(2)}) copy-start(bf16[128,16,192]{0,2,1:T(8,128)(2,1)} %param.14) | copy-start | bytes 2359300
  0.6 3.3 %slice-start = ((bf16[128,576]{0,1:T(8,128)(2,1)}), bf16[128,64]{0,1:T(8,128)(2,1)S(1)}, s32[]{:S(2)}) async-start(bf16[128,576]{0,1:T(8,128)(2,1)} %param.15), calls=%async_computation.6 | async-start | bytes 32768 | tf_op jit(solution)/shard_map/slice | solution.py:535
  0.7 30.4 %collective-permute-start = (bf16[2048,896]{1,0:T(8,128)(2,1)}, bf16[2048,896]{1,0:T(8,128)(2,1)}, u32[]{:S(2)}, u32[]{:S(2)}) collective-permute-start(bf16[2048,896]{1,0:T(8,128)(2,1)} %refs_1_.3), channel_id=1, source_target_pairs={{0,4},{4,0},{8,12},{12,8},{16,20},{20,16},{24,28},{28,24},{1,5},{5... | collective-permute-start | bytes 11010056 | tf_op jit(solution)/shard_map/ppermute | solution.py:617
  6.4 3.5 %copy-start.19 = (bf16[256,128]{1,0:T(8,128)(2,1)S(1)}, bf16[256,128]{1,0:T(8,128)(2,1)}, u32[]{:S(2)}) copy-start(bf16[256,128]{1,0:T(8,128)(2,1)} %get-tuple-element.22) | copy-start | bytes 196612
  7.8 7.3 %copy-start.7 = (f32[1,256,128]{2,1,0:T(8,128)S(1)}, f32[1,256,128]{2,1,0:T(8,128)}, u32[]{:S(2)}) copy-start(f32[1,256,128]{2,1,0:T(8,128)} %param.25) | copy-start | bytes 393220
  7.8 8.2 %copy-start.18 = (bf16[128,128]{1,0:T(8,128)(2,1)S(1)}, bf16[128,128]{1,0:T(8,128)(2,1)}, u32[]{:S(2)}) copy-start(bf16[128,128]{1,0:T(8,128)(2,1)} %get-tuple-element.21) | copy-start | bytes 98308
  11.3 19.7 %all-to-all-start = ((bf16[4,64,2048]{2,1,0:T(8,128)(2,1)}), bf16[4,64,2048]{2,1,0:T(8,128)(2,1)S(1)}, u32[]{:S(2)}, u32[]{:S(2)}) async-start(bf16[4,64,2048]{2,1,0:T(8,128)(2,1)} %bitcast.8), calls=%async_computation | async-start | bytes 2097152 | tf_op jit(solution)/shard_map/all_to_all | solution.py:559
  31.1 1.0 copy-start.1
  32.1 11.5 %copy-start.4 = (bf16[64,2048]{1,0:T(8,128)(2,1)S(1)}, bf16[64,2048]{1,0:T(8,128)(2,1)}, u32[]{:S(2)}) copy-start(bf16[64,2048]{1,0:T(8,128)(2,1)} %convolution_convert_fusion.4.refs_4_.refs_3_) | copy-start | bytes 786436
  39.1 18.1 %all-to-all-start.1 = ((bf16[4,64,1792]{2,1,0:T(8,128)(2,1)}), bf16[4,64,1792]{2,1,0:T(8,128)(2,1)}, u32[]{:S(2)}, u32[]{:S(2)}) async-start(bf16[4,64,1792]{2,1,0:T(8,128)(2,1)} %shard_map.158.refs_4_), calls=%async_computation.1 | async-start | bytes 1835008 | tf_op jit(solution)/shard_map/all_to_all | solution.py:559
  43.5 33.6 %collective-permute-start.1 = (bf16[64,2048]{1,0:T(8,128)(2,1)S(1)}, bf16[64,2048]{1,0:T(8,128)(2,1)S(1)}, u32[]{:S(2)}, u32[]{:S(2)}) collective-permute-start(bf16[64,2048]{1,0:T(8,128)(2,1)S(1)} %copy-done.4), channel_id=1, source_target_pairs={{0,8},{4,12},{8,0},{12,4},{16,24},{20,28},{24,16},{28,20},{1,9},{5... | collective-permute-start | bytes 786440 | tf_op jit(solution)/shard_map/ppermute | solution.py:569
  45.6 31.5 %collective-permute-start.2 = (bf16[64,2048]{1,0:T(8,128)(2,1)S(1)}, bf16[64,2048]{1,0:T(8,128)(2,1)S(1)}, u32[]{:S(2)}, u32[]{:S(2)}) collective-permute-start(bf16[64,2048]{1,0:T(8,128)(2,1)S(1)} %copy-done.4), channel_id=1, source_target_pairs={{0,16},{4,20},{8,24},{12,28},{16,0},{20,4},{24,8},{28,12},{1,17},{... | collective-permute-start | bytes 786440 | tf_op jit(solution)/shard_map/ppermute | solution.py:569
  47.1 30.1 %collective-permute-start.3 = (bf16[64,2048]{1,0:T(8,128)(2,1)S(1)}, bf16[64,2048]{1,0:T(8,128)(2,1)S(1)}, u32[]{:S(2)}, u32[]{:S(2)}) collective-permute-start(bf16[64,2048]{1,0:T(8,128)(2,1)S(1)} %copy-done.4), channel_id=1, source_target_pairs={{0,24},{4,28},{8,16},{12,20},{16,8},{20,12},{24,0},{28,4},{1,25},{... | collective-permute-start | bytes 786440 | tf_op jit(solution)/shard_map/ppermute | solution.py:569
  57.2 31.9 %all-to-all-start.2 = ((bf16[4,1,64,1792]{3,2,1,0:T(8,128)(2,1)}), bf16[4,1,64,1792]{3,2,1,0:T(8,128)(2,1)S(1)}, u32[]{:S(2)}, u32[]{:S(2)}) async-start(bf16[4,1,64,1792]{3,2,1,0:T(8,128)(2,1)} %bitcast.15), calls=%async_computation.2 | async-start | bytes 1835008 | tf_op jit(solution)/shard_map/all_to_all | solution.py:592
  77.1 0.8 copy-start.9
  85.6 10.3 %copy-start.21 = (bf16[1792]{0:T(1024)(128)(2,1)S(1)}, bf16[1792]{0:T(1024)(128)(2,1)}, u32[]{:S(2)}) copy-start(bf16[1792]{0:T(1024)(128)(2,1)} %param.18) | copy-start | bytes 10756
  85.6 11.4 %collective-permute-start.4 = (bf16[64,1792]{1,0:T(8,128)(2,1)}, bf16[64,1792]{1,0:T(8,128)(2,1)S(1)}, u32[]{:S(2)}, u32[]{:S(2)}) collective-permute-start(bf16[64,1792]{1,0:T(8,128)(2,1)} %get-tuple-element.26.rest_2_), channel_id=1, source_target_pairs={{0,8},{4,12},{8,0},{12,4},{16,24},{20,28},{24,16},{28,20},{1,9},{5... | collective-permute-start | bytes 688136 | tf_op jit(solution)/shard_map/ppermute | solution.py:569
  87.1 10.5 %collective-permute-start.5 = (bf16[64,1792]{1,0:T(8,128)(2,1)}, bf16[64,1792]{1,0:T(8,128)(2,1)S(1)}, u32[]{:S(2)}, u32[]{:S(2)}) collective-permute-start(bf16[64,1792]{1,0:T(8,128)(2,1)} %get-tuple-element.27.rest_3_), channel_id=1, source_target_pairs={{0,16},{4,20},{8,24},{12,28},{16,0},{20,4},{24,8},{28,12},{1,17},{... | collective-permute-start | bytes 688136 | tf_op jit(solution)/shard_map/ppermute | solution.py:569
  87.6 9.9 %collective-permute-start.6 = (bf16[64,1792]{1,0:T(8,128)(2,1)}, bf16[64,1792]{1,0:T(8,128)(2,1)S(1)}, u32[]{:S(2)}, u32[]{:S(2)}) collective-permute-start(bf16[64,1792]{1,0:T(8,128)(2,1)} %get-tuple-element.28.rest_4_), channel_id=1, source_target_pairs={{0,24},{4,28},{8,16},{12,20},{16,8},{20,12},{24,0},{28,4},{1,25},{... | collective-permute-start | bytes 688136 | tf_op jit(solution)/shard_map/ppermute | solution.py:569
  89.1 0.9 copy-start.2
  92.4 9.9 %all-to-all-start.3 = ((bf16[8,8,1792]{2,1,0:T(8,128)(2,1)}), bf16[8,8,1792]{2,1,0:T(8,128)(2,1)S(1)}, u32[]{:S(2)}, u32[]{:S(2)}) async-start(bf16[8,8,1792]{2,1,0:T(8,128)(2,1)} %bitcast.64), calls=%async_computation.3 | async-start | bytes 458752 | tf_op jit(solution)/shard_map/all_to_all | solution.py:642
  108.2 22.9 %copy-start.17 = (bf16[64,1792]{1,0:T(8,128)(2,1)S(1)}, bf16[64,1792]{1,0:T(8,128)(2,1)}, u32[]{:S(2)}) copy-start(bf16[64,1792]{1,0:T(8,128)(2,1)} %get-tuple-element.32.rest_1_) | copy-start | bytes 688132
  108.2 24.4 %copy-start.16 = (bf16[64,1792]{1,0:T(8,128)(2,1)S(1)}, bf16[64,1792]{1,0:T(8,128)(2,1)}, u32[]{:S(2)}) copy-start(bf16[64,1792]{1,0:T(8,128)(2,1)} %get-tuple-element.33.rest_2_) | copy-start | bytes 688132
  108.2 25.6 %copy-start.15 = (bf16[64,1792]{1,0:T(8,128)(2,1)S(1)}, bf16[64,1792]{1,0:T(8,128)(2,1)}, u32[]{:S(2)}) copy-start(bf16[64,1792]{1,0:T(8,128)(2,1)} %get-tuple-element.34.rest_3_) | copy-start | bytes 688132
  108.2 27.4 %copy-start.3 = (bf16[128,1792]{1,0:T(8,128)(2,1)S(1)}, bf16[128,1792]{1,0:T(8,128)(2,1)}, u32[]{:S(2)}) copy-start(bf16[128,1792]{1,0:T(8,128)(2,1)} %residual.1) | copy-start | bytes 1376260
  108.2 64.7 %copy-start.5 = (bf16[64,1792]{1,0:T(8,128)(2,1)S(1)}, bf16[64,1792]{1,0:T(8,128)(2,1)}, u32[]{:S(2)}) copy-start(bf16[64,1792]{1,0:T(8,128)(2,1)} %get-tuple-element.31.rest_0_) | copy-start | bytes 688132
  121.8 51.4 %copy-start.11 = (bf16[64,1792]{1,0:T(8,128)(2,1)S(1)}, bf16[64,1792]{1,0:T(8,128)(2,1)}, u32[]{:S(2)}) copy-start(bf16[64,1792]{1,0:T(8,128)(2,1)} %get-tuple-element.29) | copy-start | bytes 688132
  121.8 52.5 %copy-start.20 = (bf16[64,128]{1,0:T(8,128)(2,1)S(1)}, bf16[64,128]{1,0:T(8,128)(2,1)}, u32[]{:S(2)}) copy-start(bf16[64,128]{1,0:T(8,128)(2,1)} %get-tuple-element.35) | copy-start | bytes 49156
  126.3 47.9 %all-to-all-start.5 = ((bf16[32,8,1792]{2,1,0:T(8,128)(2,1)}), bf16[32,8,1792]{2,1,0:T(8,128)(2,1)S(1)}, u32[]{:S(2)}, u32[]{:S(2)}) async-start(bf16[32,8,1792]{2,1,0:T(8,128)(2,1)} %bitcast.62), calls=%async_computation.5 | async-start | bytes 1835008 | tf_op jit(solution)/shard_map/all_to_all | solution.py:673
  131.1 35.4 %collective-permute-start.7 = (bf16[64,1792]{1,0:T(8,128)(2,1)S(1)}, bf16[64,1792]{1,0:T(8,128)(2,1)S(1)}, u32[]{:S(2)}, u32[]{:S(2)}) collective-permute-start(bf16[64,1792]{1,0:T(8,128)(2,1)S(1)} %copy-done.17), channel_id=1, source_target_pairs={{0,1},{1,2},{2,3},{3,0},{4,5},{5,6},{6,7},{7,4},{8,9},{9,10},{10,1... | collective-permute-start | bytes 688136 | tf_op jit(solution)/shard_map/ppermute | solution.py:585
  132.6 38.4 %collective-permute-start.8 = (bf16[64,1792]{1,0:T(8,128)(2,1)S(1)}, bf16[64,1792]{1,0:T(8,128)(2,1)S(1)}, u32[]{:S(2)}, u32[]{:S(2)}) collective-permute-start(bf16[64,1792]{1,0:T(8,128)(2,1)S(1)} %copy-done.16), channel_id=1, source_target_pairs={{0,2},{1,3},{2,0},{3,1},{4,6},{5,7},{6,4},{7,5},{8,10},{9,11},{10,... | collective-permute-start | bytes 688136 | tf_op jit(solution)/shard_map/ppermute | solution.py:585
  133.8 39.2 %collective-permute-start.9 = (bf16[64,1792]{1,0:T(8,128)(2,1)S(1)}, bf16[64,1792]{1,0:T(8,128)(2,1)S(1)}, u32[]{:S(2)}, u32[]{:S(2)}) collective-permute-start(bf16[64,1792]{1,0:T(8,128)(2,1)S(1)} %copy-done.15), channel_id=1, source_target_pairs={{0,3},{1,0},{2,1},{3,2},{4,7},{5,4},{6,5},{7,6},{8,11},{9,8},{10,9... | collective-permute-start | bytes 688136 | tf_op jit(solution)/shard_map/ppermute | solution.py:585
  (6 other events, 4.2 us)
